TPU v7x, 256 devices: a whole 4x4x8 slice. The times are simulated.
256 devices in a mesh: band: 8 (over y, core), member: 32 (over x, z).
Axes of the slice: x: 4, y: 4, z: 8, core: 2. Of those that a mesh axis runs over, the one named last changes fastest.
Arguments:
- ensemble: bfloat16 [256, 4, 256, 1024], P('member', None, 'band'), may hold values from -6 to 6
- variance: float32 [4, 256, 1024], P(None, 'band'), may hold values from 0.25 to 4
- obs_index: int32 [32, 32768], P('member', 'band'), may hold values from 0 to 131071
- obs_value: float32 [32, 32768], P('member', 'band'), may hold values from -8 to 8
- obs_error: float32 [32, 32768], P('member', 'band'), may hold values from 0.5 to 2
- root_ranks: int32 [2], replicated, may hold values from 0 to 31
Outputs:
- increment: float32 [4, 256, 1024], P(None, 'band')
Inputs may be any that keep to these rules, and one draw needn't show every extreme that they name: `obs_index`: the position level * 32 * 1024 + row within the band * 1024 + longitude; columns b * 4096 to (b + 1) * 4096 - 1 belong to band b; positions may repeat.
All inputs are finite; a program needn't handle non-finite values.
Results may differ from a plain program's by a relative error of at most 0.0024.
Values may be sent and summed in bfloat16 or wider, within the bound.
A program may use at most 64 MiB of HBM per device.

v0:
```python
import jax
import jax.numpy as jnp
from jax import lax
from jax.sharding import Mesh
from jax.sharding import PartitionSpec as P

HALF = 8
ITERS = 2
BAND = ("band_0", "band_1")
MEMBER = ("member_0", "member_1")
BAND_MEMBER = ("band_0", "band_1", "member_0", "member_1")


huber_edge = 1.5
ensemble_share = 0.75
static_share = 0.25


def picked(x, axis, root):
    return lax.dynamic_index_in_dim(lax.all_gather(x, axis), root, 0, keepdims=False)


def from_root(x, axes, root):
    x = jnp.where(lax.axis_index(axes) == root, x, jnp.zeros_like(x))
    for axis in axes:
        x = lax.psum(x, axis)
    return x


def with_halo(x, sides, width):
    for axis, dim in sides:
        count, length = (lax.axis_size(axis), x.shape[dim])
        up = [(i, (i + 1) % count) for i in range(count - 1)]
        down = [(j, i) for i, j in up]
        last = lax.slice_in_dim(x, length - width, length, axis=dim)
        initial = lax.slice_in_dim(x, 0, width, axis=dim)
        before = lax.ppermute(last, axis, up)
        after = lax.ppermute(initial, axis, down)
        x = jnp.concatenate([before, x, after], axis=dim)
    return x


def in_blocks(x, dim, count):
    lengths = x.shape
    parts = x.reshape(*lengths[:dim], count, lengths[dim] // count, *lengths[dim + 1 :])
    return jnp.moveaxis(parts, dim, 0)


def summed_on_arrival(x, axis, dim):
    count = lax.axis_size(axis)
    parts = lax.all_to_all(in_blocks(x, dim, count), axis, 0, 0, tiled=True)
    return jnp.sum(parts, axis=0)


def one_axis_at_a_time(x, axes):
    for axis in axes:
        x = lax.psum(x, axis)
    return x


def copy_for_each(x, axis):
    count = lax.axis_size(axis)
    return lax.all_to_all(jnp.broadcast_to(x[None], (count, *x.shape)), axis, 0, 0, tiled=True)


def joined_along(parts, dim):
    lengths = list(parts.shape[1:])
    lengths[dim] *= parts.shape[0]
    return jnp.moveaxis(parts, 0, dim).reshape(lengths)


def gathered_copies(x, axis, dim):
    parts = copy_for_each(x, axis)
    return joined_along(parts, dim)


def tap_matrix(distance, radius):
    offsets = jnp.arange(-radius, radius + 1).astype(jnp.float32)
    raw = jnp.exp(-0.5 * (offsets / (0.5 * radius)) ** 2)
    norm_value = jnp.sqrt(jnp.sum(raw * raw))
    scaled = distance.astype(jnp.float32) / (0.5 * radius)
    entry = jnp.exp(-0.5 * scaled**2) / norm_value
    return jnp.where(jnp.abs(distance) <= radius, entry, 0.0).astype(jnp.bfloat16)


def lon_operator(lon_cols, radius):
    source = jnp.arange(lon_cols)[:, None]
    target = jnp.arange(lon_cols)[None, :]
    offset = (target - source) % lon_cols
    circular = jnp.minimum(offset, lon_cols - offset)
    return tap_matrix(circular, radius)


def lat_operator(out_rows, radius):
    target = jnp.arange(out_rows)[:, None]
    source = jnp.arange(out_rows + 2 * radius)[None, :]
    return tap_matrix(source - radius - target, radius)


def apply_rows(matrix, padded):
    return jnp.einsum("ij,bjk->bik", matrix, padded, preferred_element_type=jnp.float32)


def make_gradient(field, positions, values, errors):
    departure = values - field.reshape(-1)[positions]
    weight = huber_edge / jnp.maximum(jnp.abs(departure / errors), huber_edge)
    flat = (
        jnp.zeros((field.size,), jnp.float32)
        .at[positions]
        .add(weight * departure / (errors * errors))
    )
    return (weight, flat.reshape(field.shape))


def local(ensemble, variance, obs_index, obs_value, obs_error, root_ranks):
    members_here, levels, lat_rows, lon_cols = ensemble.shape
    stacked_rows = members_here * levels
    band_pos = lax.axis_index(BAND)
    member_pos = lax.axis_index(MEMBER)
    all_rows = lax.axis_size(BAND) * lat_rows
    members = members_here * lax.axis_size(MEMBER)
    lon_matrix = lon_operator(lon_cols, HALF)
    lat_matrix = lat_operator(lat_rows, HALF)
    wide_matrix = lat_operator(lat_rows + 2 * HALF, HALF)
    global_row = band_pos * lat_rows - HALF + jnp.arange(lat_rows + 2 * HALF)
    keep_rows = (global_row >= 0) & (global_row < all_rows)
    positions = obs_index[0]
    values = obs_value[0]
    errors = obs_error[0]
    field = jnp.zeros((levels, lat_rows, lon_cols), jnp.float32)
    for iteration in range(ITERS):
        block = root_ranks[iteration]
        use_places = picked(positions, MEMBER, block)
        use_values, use_errors = (
            from_root(values, MEMBER, block),
            from_root(errors, MEMBER, block),
        )
        weight, gradient = make_gradient(field, use_places, use_values, use_errors)
        mixed = (ensemble.astype(jnp.float32) * gradient[None]).astype(jnp.bfloat16)
        mixed = mixed.reshape(stacked_rows, lat_rows, lon_cols)
        first = jnp.dot(mixed, lon_matrix, preferred_element_type=jnp.float32).astype(jnp.bfloat16)
        padded = with_halo(first, ((BAND, 1),), 2 * HALF)
        widened = apply_rows(wide_matrix, padded)
        widened = jnp.where(keep_rows[None, :, None], widened, 0.0).astype(jnp.bfloat16)
        second = jnp.dot(widened, lon_matrix, preferred_element_type=jnp.float32).astype(
            jnp.bfloat16
        )
        second = apply_rows(lat_matrix, second)
        second = second.reshape(members_here, levels, lat_rows, lon_cols)
        spread = jnp.sum(ensemble.astype(jnp.float32) * second, axis=0)
        piece_rows = levels * lat_rows // lax.axis_size(MEMBER)
        start = member_pos * piece_rows
        summed = summed_on_arrival(spread.reshape(levels * lat_rows, lon_cols), MEMBER, 0)
        var_piece = lax.dynamic_slice_in_dim(
            variance.reshape(levels * lat_rows, lon_cols), start, piece_rows, 0
        )
        grad_piece = lax.dynamic_slice_in_dim(
            gradient.reshape(levels * lat_rows, lon_cols), start, piece_rows, 0
        )
        field_piece = lax.dynamic_slice_in_dim(
            field.reshape(levels * lat_rows, lon_cols), start, piece_rows, 0
        )
        dir_piece = ensemble_share * summed / (members - 1) + static_share * var_piece * grad_piece
        piece_sums = (
            one_axis_at_a_time(jnp.sum(grad_piece * dir_piece), BAND_MEMBER),
            one_axis_at_a_time(jnp.sum(field_piece * grad_piece), BAND_MEMBER),
        )
        direction = gathered_copies(dir_piece, MEMBER, 0).reshape(levels, lat_rows, lon_cols)
        reached = direction.reshape(-1)[use_places]
        curve_local = jnp.sum(weight * reached * reached / (use_errors * use_errors))
        is_root = (member_pos == block).astype(jnp.float32)
        curve = one_axis_at_a_time(is_root * curve_local, BAND_MEMBER)
        along, back = piece_sums
        field = field + (along - back) / (along + curve) * direction
    return field


def solution(mesh):
    split = Mesh(mesh.devices.reshape(4, 2, 4, 8), ("band_0", "band_1", "member_0", "member_1"))
    in_specs = (
        P(MEMBER, None, BAND, None),
        P(None, BAND, None),
        P(MEMBER, BAND),
        P(MEMBER, BAND),
        P(MEMBER, BAND),
        P(),
    )
    out_specs = P(None, BAND, None)
    return jax.shard_map(local, mesh=split, in_specs=in_specs, out_specs=out_specs, check_vma=False)
```

profile of v0, /device:TPU:1, one launch (start us, length us, event | category | flops | bytes accessed | tf_op | source)
XLA Modules:
  0.0 527.7 jit_solution(9792387134905237062)
XLA Ops:
  6.0 41.4 %all-gather = s32[32,1,4096]{2,1,0:T(1,128)S(1)} all-gather(s32[1,1,4096]{2,1,0:T(1,128)} %bitcast.89), channel_id=1, replica_groups=mesh['band_0'=4,'band_1'=2,'member_0'=4,'member_1'=8] {'member_0','membe..., dimensions={0}, use_global_device_ids=true | all-gather | bytes 540672 | tf_op jit(solution)/shard_map/all_gather | solution.py:20
  49.6 12.9 %all-reduce.5 = (f32[4096]{0:T(1024)S(1)}, f32[4096]{0:T(1024)S(1)}) all-reduce(f32[4096]{0:T(1024)S(1)} %bitcast.83, f32[4096]{0:T(1024)S(1)} %bitcast.84), channel_id=1, replica_groups=mesh['band_0'=4,'band_1'=2,'member_0'=4,'member_1'=8] {'member_0'}, use_global_device_ids=true, to_apply=%region_2.3 | all-reduce | flops 8192 | bytes 65536 | tf_op jit(solution)/shard_map/psum | solution.py:26
  62.5 20.7 %all-reduce.2 = (f32[4096]{0:T(1024)S(1)}, f32[4096]{0:T(1024)S(1)}) all-reduce(f32[4096]{0:T(1024)S(1)} %get-tuple-element.27, f32[4096]{0:T(1024)S(1)} %get-tuple-element.28), channel_id=1, replica_groups=mesh['band_0'=4,'band_1'=2,'member_0'=4,'member_1'=8] {'member_1'}, use_global_device_ids=true, to_apply=%region_3.4 | all-reduce | flops 8192 | bytes 65536 | tf_op jit(solution)/shard_map/psum | solution.py:26
  83.3 23.0 %gather_fusion = f32[4096]{0:T(1024)S(1)} fusion(f32[131072]{0:T(1024)S(1)} %broadcast.127, s32[4096]{0:T(1024)S(1)} %broadcast_clamp_fusion.1), kind=kCustom, calls=%fused_computation | custom fusion | bytes 49152 | tf_op jit(solution)/shard_map/gather | solution.py:105
  106.3 22.0 %scatter_custom_fusion = f32[131072]{0:T(1024)S(1)} fusion(s32[4096]{0:T(1024)S(1)} %bitcast.88, f32[4096]{0:T(1024)S(1)} %multiply_divide_fusion.1, f32[]{:T(128)} %constant.32.clone.1), kind=kCustom, calls=%fused_computation.72 | custom fusion | flops 4096 | bytes 524292 | tf_op jit(solution)/shard_map/scatter-add | solution.py:110
  138.1 26.5 %collective-permute-start = (bf16[32,16,1024]{2,1,0:T(8,128)(2,1)}, bf16[32,16,1024]{2,1,0:T(8,128)(2,1)}, u32[]{:S(2)}, u32[]{:S(2)}) collective-permute-start(bf16[32,16,1024]{2,1,0:T(8,128)(2,1)} %get-tuple-element.45), channel_id=1, source_target_pairs={{0,32},{32,64},{64,96},{96,128},{128,160},{160,192},{192,224},{1,3... | collective-permute-start | bytes 3145736 | tf_op jit(solution)/shard_map/ppermute | solution.py:37
  166.7 9.9 %collective-permute-done = bf16[32,16,1024]{2,1,0:T(8,128)(2,1)} collective-permute-done((bf16[32,16,1024]{2,1,0:T(8,128)(2,1)}, bf16[32,16,1024]{2,1,0:T(8,128)(2,1)}, u32[]{:S(2)}, u32[]{:S(2)}) %collective-permute-start) | collective-permute-done | bytes 1048608 | tf_op jit(solution)/shard_map/ppermute | solution.py:37
  205.2 10.5 %all-to-all-done = f32[32,4,1024]{2,1,0:T(4,128)S(1)} async-done(((f32[32,4,1024]{2,1,0:T(4,128)}), f32[32,4,1024]{2,1,0:T(4,128)S(1)}, u32[]{:S(2)}, u32[]{:S(2)}) %all-to-all-start) | async-done | bytes 524320 | tf_op jit(solution)/shard_map/all_to_all | solution.py:51
  223.7 11.4 %all-to-all-done.1 = f32[32,4,1024]{2,1,0:T(4,128)S(1)} async-done(((f32[32,4,1024]{2,1,0:T(4,128)}), f32[32,4,1024]{2,1,0:T(4,128)S(1)}, u32[]{:S(2)}, u32[]{:S(2)}) %all-to-all-start.1) | async-done | bytes 524320 | tf_op jit(solution)/shard_map/all_to_all | solution.py:63
  235.1 23.0 %gather_fusion.1 = f32[4096]{0:T(1024)S(1)} fusion(f32[131072]{0:T(1024)S(1)} %bitcast.67, s32[4096]{0:T(1024)S(1)} %broadcast_clamp_fusion.1), kind=kCustom, calls=%fused_computation.1 | custom fusion | bytes 49152 | tf_op jit(solution)/shard_map/gather | solution.py:169
  259.5 15.6 %all-reduce.7 = (f32[]{:T(128)}, f32[]{:T(128)}, f32[]{:T(128)}) all-reduce(f32[]{:T(128)} %get-tuple-element.8, f32[]{:T(128)} %get-tuple-element.7, f32[]{:T(128)S(6)} %mul.170), channel_id=1, replica_groups=mesh['band_0'=4,'band_1'=2,'member_0'=4,'member_1'=8] {'band_0'}, use_global_device_ids=true, to_apply=%region_9.10 | all-reduce | flops 3 | bytes 24 | tf_op jit(solution)/shard_map/psum | solution.py:57
  283.5 13.4 %all-reduce.4 = (f32[]{:T(128)}, f32[]{:T(128)}, f32[]{:T(128)}, f32[4096]{0:T(1024)S(1)}, f32[4096]{0:T(1024)S(1)}) all-reduce(f32[]{:T(128)} %get-tuple-element.38, f32[]{:T(128)} %get-tuple-element.39, f32[]{:T(128)} %get-tuple-element.40, ...), channel_id=1, replica_groups=mesh['band_0'=4,'band_1'=2,'member_0'=4,'member_1'=8] {'member_0'}, use_global_device_ids=true, to_apply=%region_11.12 | all-reduce | flops 8195 | bytes 65560 | tf_op jit(solution)/shard_map/psum | solution.py:57
  296.8 23.9 %all-reduce.1 = (f32[]{:T(128)}, f32[]{:T(128)}, f32[]{:T(128)}, f32[4096]{0:T(1024)S(1)}, f32[4096]{0:T(1024)S(1)}) all-reduce(f32[]{:T(128)} %get-tuple-element.22, f32[]{:T(128)} %get-tuple-element.23, f32[]{:T(128)} %get-tuple-element.24, ...), channel_id=1, replica_groups=mesh['band_0'=4,'band_1'=2,'member_0'=4,'member_1'=8] {'member_1'}, use_global_device_ids=true, to_apply=%region_12.13 | all-reduce | flops 8195 | bytes 65560 | tf_op jit(solution)/shard_map/psum | solution.py:57
  323.4 23.0 %gather_fusion.2 = f32[4096]{0:T(1024)S(1)} fusion(f32[131072]{0:T(1024)S(1)} %broadcast_multiply_fusion, s32[4096]{0:T(1024)S(1)} %broadcast_clamp_fusion), kind=kCustom, calls=%fused_computation.2 | custom fusion | bytes 49152 | tf_op jit(solution)/shard_map/gather | solution.py:105
  346.4 22.3 %scatter_custom_fusion.1 = f32[131072]{0:T(1024)S(1)} fusion(s32[4096]{0:T(1024)S(1)} %bitcast.86, f32[4096]{0:T(1024)S(1)} %multiply_divide_fusion, f32[]{:T(128)} %constant.32.clone.1), kind=kCustom, calls=%fused_computation.70 | custom fusion | flops 4096 | bytes 524292 | tf_op jit(solution)/shard_map/scatter-add | solution.py:110
  375.1 13.9 %collective-permute-start.2 = (bf16[32,16,1024]{2,1,0:T(8,128)(2,1)S(1)}, bf16[32,16,1024]{2,1,0:T(8,128)(2,1)S(1)}, u32[]{:S(2)}, u32[]{:S(2)}) collective-permute-start(bf16[32,16,1024]{2,1,0:T(8,128)(2,1)S(1)} %get-tuple-element.43), channel_id=1, source_target_pairs={{0,32},{32,64},{64,96},{96,128},{128,160},{160,192},{192,224},{1,3... | collective-permute-start | bytes 3145736 | tf_op jit(solution)/shard_map/ppermute | solution.py:37
  390.9 9.8 %collective-permute-done.2 = bf16[32,16,1024]{2,1,0:T(8,128)(2,1)S(1)} collective-permute-done((bf16[32,16,1024]{2,1,0:T(8,128)(2,1)S(1)}, bf16[32,16,1024]{2,1,0:T(8,128)(2,1)S(1)}, u32[]{:S(2)}, u32[]{:S(2)}) %collective-permute-start.2) | collective-permute-done | bytes 1048608 | tf_op jit(solution)/shard_map/ppermute | solution.py:37
  407.6 8.8 %fusion.26 = f32[32,1024,32]{1,2,0:T(8,128)} fusion(bf16[32,1024,48]{1,2,0:T(8,128)(2,1)} %fusion.11, pred[48]{0:T(512)(128)(4,1)S(1)} %compare_and_fusion, f32[]{:T(128)S(6)} %sqrt.2, s32[48]{0:T(128)S(1)} %iota_add_fusion), kind=kOutput, calls=%fused_computation.42 | convolution fusion | flops 3349167104 | bytes 7340276 | tf_op jit(solution)/shard_map/ij,bjk->bik/dot_general | solution.py:101
  426.4 11.0 %all-to-all-done.2 = f32[32,4,1024]{2,1,0:T(4,128)S(1)} async-done(((f32[32,4,1024]{2,1,0:T(4,128)}), f32[32,4,1024]{2,1,0:T(4,128)S(1)}, u32[]{:S(2)}, u32[]{:S(2)}) %all-to-all-start.2) | async-done | bytes 524320 | tf_op jit(solution)/shard_map/all_to_all | solution.py:51
  439.1 16.7 %all_to_all.20 = f32[32,4,1024]{2,1,0:T(4,128)S(1)} all-to-all(f32[32,4,1024]{2,1,0:T(4,128)S(1)} %broadcast_in_dim.60), channel_id=1, replica_groups=mesh['band_0'=4,'band_1'=2,'member_0'=4,'member_1'=8] {'member_0','membe..., dimensions={0} | all-to-all | bytes 1048576 | tf_op jit(solution)/shard_map/all_to_all | solution.py:63
  455.8 23.0 %gather_fusion.3 = f32[4096]{0:T(1024)S(1)} fusion(f32[131072]{0:T(1024)S(1)} %bitcast.69, s32[4096]{0:T(1024)S(1)} %broadcast_clamp_fusion), kind=kCustom, calls=%fused_computation.3 | custom fusion | bytes 49152 | tf_op jit(solution)/shard_map/gather | solution.py:169
  480.0 14.2 %all-reduce.6 = (f32[]{:T(128)}, f32[]{:T(128)}, f32[]{:T(128)}) all-reduce(f32[]{:T(128)} %get-tuple-element.6, f32[]{:T(128)} %get-tuple-element.5, f32[]{:T(128)S(6)} %mul.187), channel_id=1, replica_groups=mesh['band_0'=4,'band_1'=2,'member_0'=4,'member_1'=8] {'band_0'}, use_global_device_ids=true, to_apply=%region_31.32 | all-reduce | flops 3 | bytes 24 | tf_op jit(solution)/shard_map/psum | solution.py:57
  494.2 8.9 %all-reduce.8 = (f32[]{:T(128)}, f32[]{:T(128)}, f32[]{:T(128)}) all-reduce(f32[]{:T(128)} %get-tuple-element.29, f32[]{:T(128)} %get-tuple-element.30, f32[]{:T(128)} %get-tuple-element.31), channel_id=1, replica_groups=mesh['band_0'=4,'band_1'=2,'member_0'=4,'member_1'=8] {'band_1'}, use_global_device_ids=true, to_apply=%region_32.33 | all-reduce | flops 3 | bytes 24 | tf_op jit(solution)/shard_map/psum | solution.py:57
  510.3 13.7 %all-reduce = (f32[]{:T(128)}, f32[]{:T(128)}, f32[]{:T(128)}) all-reduce(f32[]{:T(128)} %get-tuple-element.19, f32[]{:T(128)} %get-tuple-element.20, f32[]{:T(128)} %get-tuple-element.21), channel_id=1, replica_groups=mesh['band_0'=4,'band_1'=2,'member_0'=4,'member_1'=8] {'member_1'}, use_global_device_ids=true, to_apply=%region_34.35 | all-reduce | flops 3 | bytes 24 | tf_op jit(solution)/shard_map/psum | solution.py:57
  (61 shorter events, 95.4 us)
Async XLA Ops:
  83.3 45.8 %copy-start = (bf16[8,4,32,1024]{3,2,1,0:T(8,128)(2,1)S(1)}, bf16[8,4,32,1024]{3,2,1,0:T(8,128)(2,1)}, u32[]{:S(2)}) copy-start(bf16[8,4,32,1024]{3,2,1,0:T(8,128)(2,1)} %param.6) | copy-start | bytes 6291460
  135.2 1.4 copy-start.3
  138.1 38.6 %collective-permute-start = (bf16[32,16,1024]{2,1,0:T(8,128)(2,1)}, bf16[32,16,1024]{2,1,0:T(8,128)(2,1)}, u32[]{:S(2)}, u32[]{:S(2)}) collective-permute-start(bf16[32,16,1024]{2,1,0:T(8,128)(2,1)} %get-tuple-element.45), channel_id=1, source_target_pairs={{0,32},{32,64},{64,96},{96,128},{128,160},{160,192},{192,224},{1,3... | collective-permute-start | bytes 3145736 | tf_op jit(solution)/shard_map/ppermute | solution.py:37
  164.6 16.4 %collective-permute-start.1 = (bf16[32,16,1024]{2,1,0:T(8,128)(2,1)}, bf16[32,16,1024]{2,1,0:T(8,128)(2,1)}, u32[]{:S(2)}, u32[]{:S(2)}) collective-permute-start(bf16[32,16,1024]{2,1,0:T(8,128)(2,1)} %get-tuple-element.46), channel_id=1, source_target_pairs={{32,0},{64,32},{96,64},{128,96},{160,128},{192,160},{224,192},{33,... | collective-permute-start | bytes 3145736 | tf_op jit(solution)/shard_map/ppermute | solution.py:38
  198.5 17.2 %all-to-all-start = ((f32[32,4,1024]{2,1,0:T(4,128)}), f32[32,4,1024]{2,1,0:T(4,128)S(1)}, u32[]{:S(2)}, u32[]{:S(2)}) async-start(f32[32,4,1024]{2,1,0:T(4,128)} %reshape_reshape.15), calls=%async_computation | async-start | bytes 1048576 | tf_op jit(solution)/shard_map/all_to_all | solution.py:51
  218.2 16.9 %all-to-all-start.1 = ((f32[32,4,1024]{2,1,0:T(4,128)}), f32[32,4,1024]{2,1,0:T(4,128)S(1)}, u32[]{:S(2)}, u32[]{:S(2)}) async-start(f32[32,4,1024]{2,1,0:T(4,128)} %broadcast_in_dim.59), calls=%async_computation.1 | async-start | bytes 1048576 | tf_op jit(solution)/shard_map/all_to_all | solution.py:63
  235.1 23.1 %copy-start.1 = (f32[32,4,1024]{2,1,0:T(4,128)}, f32[32,4,1024]{2,1,0:T(4,128)S(1)}, u32[]{:S(2)}) copy-start(f32[32,4,1024]{2,1,0:T(4,128)S(1)} %all-to-all-done.1) | copy-start | bytes 1572868
  375.1 25.6 %collective-permute-start.2 = (bf16[32,16,1024]{2,1,0:T(8,128)(2,1)S(1)}, bf16[32,16,1024]{2,1,0:T(8,128)(2,1)S(1)}, u32[]{:S(2)}, u32[]{:S(2)}) collective-permute-start(bf16[32,16,1024]{2,1,0:T(8,128)(2,1)S(1)} %get-tuple-element.43), channel_id=1, source_target_pairs={{0,32},{32,64},{64,96},{96,128},{128,160},{160,192},{192,224},{1,3... | collective-permute-start | bytes 3145736 | tf_op jit(solution)/shard_map/ppermute | solution.py:37
  389.0 16.1 %collective-permute-start.3 = (bf16[32,16,1024]{2,1,0:T(8,128)(2,1)S(1)}, bf16[32,16,1024]{2,1,0:T(8,128)(2,1)S(1)}, u32[]{:S(2)}, u32[]{:S(2)}) collective-permute-start(bf16[32,16,1024]{2,1,0:T(8,128)(2,1)S(1)} %get-tuple-element.44), channel_id=1, source_target_pairs={{32,0},{64,32},{96,64},{128,96},{160,128},{192,160},{224,192},{33,... | collective-permute-start | bytes 3145736 | tf_op jit(solution)/shard_map/ppermute | solution.py:38
  416.4 9.7 %copy-start.2 = (f32[32,4,1024]{2,1,0:T(4,128)S(1)}, f32[32,4,1024]{2,1,0:T(4,128)}, u32[]{:S(2)}) copy-start(f32[32,4,1024]{2,1,0:T(4,128)} %copy-done.1) | copy-start | bytes 1572868
  422.1 15.3 %all-to-all-start.2 = ((f32[32,4,1024]{2,1,0:T(4,128)}), f32[32,4,1024]{2,1,0:T(4,128)S(1)}, u32[]{:S(2)}, u32[]{:S(2)}) async-start(f32[32,4,1024]{2,1,0:T(4,128)} %reshape_reshape.17), calls=%async_computation.2 | async-start | bytes 1048576 | tf_op jit(solution)/shard_map/all_to_all | solution.py:51
where the time goes:
time: 533 us; the launch traced here: 528 us
  blocking collectives  197 us (37%)
  local copies, waits for them, and re-layouts  103 us (19%)
  waiting for transfers between devices  61.4 us (12%)
  starting transfers between devices  59.6 us (11%)
  other arithmetic  58.2 us (11%)
  matrix products  36 us (7%)
  between operations  12.8 us (2%)
    psum x8, blocking collectives, one_axis_at_a_time(): x = lax.psum(x, axis)  105 us
    gather x2, local copies, waits for them, and re-layouts, make_gradient(): departure = values - field.reshape(-1)[positions]  46.1 us
    gather x2, local copies, waits for them, and re-layouts, local(): reached = direction.reshape(-1)[use_places]  46.1 us
    scatter-add x2, other arithmetic, make_gradient(): flat = jnp.zeros((field.size,), jnp.float32).at[positions].add(weight * d...  44.3 us
    all_gather x1, blocking collectives, picked(): lax.all_gather(x, axis)  41.4 us
    ppermute x2, starting transfers between devices, with_halo(): before = lax.ppermute(last, axis, up)  40.4 us
    psum x2, blocking collectives, from_root(): x = lax.psum(x, axis)  33.6 us
    dot_general x4, matrix products, apply_rows(): jnp.einsum('ij,bjk->bik', matrix, padded, preferred_element_type=jnp.floa...  24.9 us
  transfers between devices with their start and end apart: 7, of which 7 were waited for; matrix products, arithmetic and copies ran while one was open for 0% of the time, Pallas kernels for 0%

commit v1 on v0

v1 whole, which is shorter than its diff:
```python
import functools
import math

import jax
import jax.numpy as jnp
from jax import lax
from jax.experimental import pallas as pl
from jax.experimental.pallas import tpu as pltpu
from jax.sharding import PartitionSpec as P

HALF = 8
ITERS = 2
LANE = 128
HALO = 2 * HALF
BLK = 256
QUAD = 4
GROUP = 4

huber_edge = 1.5
ensemble_share = 0.75
static_share = 0.25

F32 = jnp.float32
BF16 = jnp.bfloat16


def taps(distance, keep):
    raw = [math.exp(-0.5 * (k / (0.5 * HALF)) ** 2) for k in range(-HALF, HALF + 1)]
    norm = math.sqrt(sum(r * r for r in raw))
    scaled = distance.astype(F32) / (0.5 * HALF)
    entry = jnp.exp(-0.5 * scaled * scaled) / norm
    keep = keep & (jnp.abs(distance) <= HALF)
    return jnp.where(keep, entry, 0.0).astype(BF16)


def iota(shape, dim):
    return lax.broadcasted_iota(jnp.int32, shape, dim)


def split(x):
    hi = x.astype(BF16).astype(F32)
    return hi, x - hi


def kernel(
    n_band, n_member, members_here, levels, lat, lon,
    root_ref, ens_ref, var_ref, idx_ref, val_ref, err_ref, out_ref,
    ext, wlon, lat1, lat2, send_obs, got_obs, obs, hot, grad, grad2, gpad,
    xpad, ypad, zpad, vpad, spread, arrived, varp, direc, split_dir,
    sums, band_sums, total_sums, member_sums,
    own_sem, ens_send, ens_recv, obs_send, obs_recv, halo_send, halo_recv,
    rs_send, rs_recv, ag_send, ag_recv, sc_send, sc_recv,
):
    me = lax.axis_index("member")
    band = lax.axis_index("band")
    rest = n_member - 1
    cols = lon // LANE
    wide = lat + 2 * HALO
    mid = lat + 2 * HALF
    rows = levels * lat
    up = lax.rem(band + 1, n_band)
    down = lax.rem(band + n_band - 1, n_band)
    my_row = pl.multiple_of((me // cols) * 8, 8)
    my_col = pl.multiple_of((me % cols) * LANE, LANE)

    def remote(src, dst, send, recv, to_band, to_member):
        return pltpu.make_async_remote_copy(
            src_ref=src, dst_ref=dst, send_sem=send, recv_sem=recv,
            device_id=(to_band, to_member), device_id_type=pl.DeviceIdType.MESH,
        )

    def drain(ref, sem):
        pltpu.make_async_copy(ref, ref, sem).wait()

    def to_members(start):
        def body(k, carry):
            start(k, lax.rem(me + k, n_member))
            return carry
        lax.fori_loop(1, n_member, body, 0)

    barrier = pltpu.get_barrier_semaphore()

    def greet_member(k, peer):
        pl.semaphore_signal(barrier, inc=1, device_id=(band, peer), device_id_type=pl.DeviceIdType.MESH)

    to_members(greet_member)

    def greet_band(k, carry):
        pl.semaphore_signal(
            barrier, inc=1, device_id=(lax.rem(band + k, n_band), me), device_id_type=pl.DeviceIdType.MESH
        )
        return carry

    lax.fori_loop(1, n_band, greet_band, 0)

    own = pltpu.make_async_copy(ens_ref, ext.at[:, :, pl.ds(HALO, lat), :], own_sem.at[0])
    own.start()
    own_var = pltpu.make_async_copy(
        var_ref.at[:, pl.ds(my_row, 8), pl.ds(my_col, LANE)], varp, own_sem.at[1]
    )
    own_var.start()

    flags = [(root_ref[it] == me).astype(F32) for it in range(ITERS)]
    for j in range(n_member):
        at = pl.ds(j * LANE, LANE)
        parts = [idx_ref[0:1, at].astype(F32), val_ref[0:1, at], err_ref[0:1, at]]
        lines = [part * flags[it] for it in range(ITERS) for part in parts]
        send_obs[j] = jnp.concatenate(lines + [jnp.zeros((2, LANE), F32)], axis=0)

    pl.semaphore_wait(barrier, n_member - 1 + n_band - 1)

    to_members(
        lambda k, peer: remote(
            send_obs.at[peer], got_obs.at[k - 1], obs_send.at[0], obs_recv.at[0], band, peer
        ).start()
    )
    ens_up = remote(
        ens_ref.at[:, :, pl.ds(lat - HALO, HALO), :], ext.at[:, :, pl.ds(0, HALO), :],
        ens_send.at[0], ens_recv.at[0], up, me,
    )
    ens_down = remote(
        ens_ref.at[:, :, pl.ds(0, HALO), :], ext.at[:, :, pl.ds(HALO + lat, HALO), :],
        ens_send.at[1], ens_recv.at[1], down, me,
    )
    ens_up.start()
    ens_down.start()

    shape = (2 * BLK, BLK)
    wlon[...] = taps(iota(shape, 1) - iota(shape, 0) + LANE, iota(shape, 0) >= 0)
    shape = (QUAD * mid, QUAD * wide)
    target, source = iota(shape, 0), iota(shape, 1)
    row_out = band * lat - HALF + target % mid
    row_in = band * lat - HALO + source % wide
    all_rows = n_band * lat
    lat1[...] = taps(
        row_in - row_out,
        (target // mid == source // wide)
        & (row_out >= 0) & (row_out < all_rows) & (row_in >= 0) & (row_in < all_rows),
    )
    shape = (QUAD * lat, QUAD * mid)
    target, source = iota(shape, 0), iota(shape, 1)
    lat2[...] = taps(source % mid - HALF - target % lat, target // lat == source // mid)

    drain(got_obs, obs_recv.at[0])
    obs[me] = send_obs[me] + jnp.sum(got_obs[...], axis=0)
    to_members(
        lambda k, peer: remote(
            obs.at[me], obs.at[me], obs_send.at[1], obs_recv.at[1], band, peer
        ).start()
    )
    drain(got_obs, obs_recv.at[1])

    groups = n_member // GROUP
    width = GROUP * LANE

    def line(g, which):
        return jnp.concatenate([obs[g * GROUP + j, which : which + 1, :] for j in range(GROUP)], axis=1)

    def build_hot(it):
        def body(g, carry):
            column = line(g, 3 * it).astype(jnp.int32) % lon
            for r in range(0, lon, LANE):
                hit = iota((LANE, width), 0) + r == column
                hot[g, r : r + LANE, :] = jnp.where(hit, 1.0, 0.0).astype(BF16)
            return carry
        lax.fori_loop(0, groups, body, 0)

    nt = (((1,), (1,)), ((), ()))

    def build_gradient(it, step):
        grad[...] = jnp.zeros_like(grad)
        grad2[...] = jnp.zeros_like(grad2)

        def body(g, carry):
            place = line(g, 3 * it).astype(jnp.int32)
            values = line(g, 3 * it + 1)
            errors = line(g, 3 * it + 2)
            row = place // lon
            departure = values
            if it > 0:
                level, in_level = row // lat, row % lat
                line_of = (in_level // 8) * (8 * levels) + level * 8 + in_level % 8
                found = jnp.dot(split_dir[...], hot[g], preferred_element_type=F32)
                found = found[:rows] + found[rows:]
                reached = jnp.sum(jnp.where(iota((rows, width), 0) == line_of, found, 0.0), axis=0, keepdims=True)
                departure = values - step * reached
            weight = huber_edge / jnp.maximum(jnp.abs(departure / errors), huber_edge)
            square = errors * errors
            hit = iota((rows, width), 0) == row
            terms = [jnp.where(hit, part, 0.0).astype(BF16) for part in split(weight * departure / square)]
            grad[...] += lax.dot_general(jnp.concatenate(terms, axis=0), hot[g], nt, preferred_element_type=F32)
            mine = iota((8 * levels, width), 0)
            hit = (mine // 8) * lat + my_row + mine % 8 == row
            terms = [jnp.where(hit, part, 0.0).astype(BF16) for part in split(weight / square)]
            grad2[...] += lax.dot_general(
                jnp.concatenate(terms, axis=0), hot[g, pl.ds(my_col, LANE), :], nt, preferred_element_type=F32
            )
            return carry

        lax.fori_loop(0, groups, body, 0)
        for level in range(levels):
            a, b = level * lat, rows + level * lat
            gpad[it, level, HALO : HALO + lat, :] = grad[a : a + lat, :] + grad[b : b + lat, :]

    def lon_filter(padded, store):
        for c in range(0, lon, BLK):
            at = slice(c, c + BLK)
            store(at, jnp.dot(padded[:, c : c + 2 * BLK], wlon[...], preferred_element_type=F32).astype(BF16))

    def put_padded(ref, at, block):
        ref[:, LANE + at.start : LANE + at.stop] = block
        if at.start == 0:
            ref[:, LANE + lon :] = block[:, :LANE]
        if at.stop == lon:
            ref[:, :LANE] = block[:, block.shape[1] - LANE :]

    def filters(it, level):
        for h in range(members_here // QUAD):
            who = slice(h * QUAD, (h + 1) * QUAD)
            xs, ys, zs, vs = xpad.at[h], ypad.at[h], zpad.at[h], vpad.at[h]
            for c in range(0, lon, BLK):
                at = slice(c, c + BLK)
                mixed = ext[who, level, :, at].astype(F32) * gpad[it, level, :, at][None]
                put_padded(xs, at, mixed.astype(BF16).reshape(QUAD * wide, BLK))

            def store_y(at, block):
                ys[:, at] = block

            lon_filter(xs, store_y)
            for c in range(0, lon, BLK):
                at = slice(c, c + BLK)
                put_padded(zs, at, jnp.dot(lat1[...], ys[:, at], preferred_element_type=F32).astype(BF16))

            def store_v(at, block):
                vs[:, at] = block

            lon_filter(zs, store_v)
            for c in range(0, lon, BLK):
                at = slice(c, c + BLK)
                second = jnp.dot(lat2[...], vs[:, at], preferred_element_type=F32).reshape(QUAD, lat, BLK)
                part = jnp.sum(ext[who, level, HALO : HALO + lat, at].astype(F32) * second, axis=0)
                if h == 0:
                    spread[it, level, :, at] = part
                else:
                    spread[it, level, :, at] += part

    steps = []
    fields = []
    build_hot(0)
    for it in range(ITERS):
        build_gradient(it, steps[-1] if steps else None)
        halo_up = remote(
            gpad.at[it, :, pl.ds(lat, HALO), :], gpad.at[it, :, pl.ds(0, HALO), :],
            halo_send.at[it, 0], halo_recv.at[it, 0], up, me,
        )
        halo_down = remote(
            gpad.at[it, :, pl.ds(HALO, HALO), :], gpad.at[it, :, pl.ds(HALO + lat, HALO), :],
            halo_send.at[it, 1], halo_recv.at[it, 1], down, me,
        )
        halo_up.start()
        halo_down.start()
        if it == 0:
            own.wait()
            own_var.wait()
            ens_up.wait()
            ens_down.wait()
        halo_up.wait()
        halo_down.wait()

        def level_body(level, carry):
            filters(it, level)

            def send(k, peer):
                row = pl.multiple_of((peer // cols) * 8, 8)
                col = pl.multiple_of((peer % cols) * LANE, LANE)
                remote(
                    spread.at[it, level, pl.ds(row, 8), pl.ds(col, LANE)], arrived.at[it, level, k - 1],
                    rs_send.at[it, level], rs_recv.at[it, level], band, peer,
                ).start()

            to_members(send)
            return carry

        lax.fori_loop(0, levels, level_body, 0)

        along = jnp.zeros((8, LANE), F32)
        back = jnp.zeros((8, LANE), F32)
        curve = jnp.zeros((8, LANE), F32)
        pieces = []
        for level in range(levels):
            drain(arrived.at[it, level], rs_recv.at[it, level])
            summed = spread[it, level, pl.ds(my_row, 8), pl.ds(my_col, LANE)] + jnp.sum(arrived[it, level], axis=0)
            g = gpad[it, level, pl.ds(HALO + my_row, 8), pl.ds(my_col, LANE)]
            d = ensemble_share * summed / (members_here * n_member - 1) + static_share * varp[level] * g
            a = level * 8
            c = grad2[a : a + 8, :] + grad2[a + 8 * levels : a + 8 * levels + 8, :]
            along += g * d
            curve += c * d * d
            if it > 0:
                back += fields[-1][level] * g
            direc[it, me // cols, a : a + 8, pl.ds(my_col, LANE)] = d
            pieces.append(d)
        sums[it] = jnp.concatenate(
            [jnp.sum(x, axis=0, keepdims=True) for x in (along, back, curve)] + [jnp.zeros((5, LANE), F32)], axis=0
        )

        def send_sums(k, carry):
            remote(
                sums.at[it], band_sums.at[it, k - 1], sc_send.at[it, 0], sc_recv.at[it, 0],
                lax.rem(band + k, n_band), me,
            ).start()
            return carry

        lax.fori_loop(1, n_band, send_sums, 0)

        def send_piece(k, peer):
            piece = direc.at[it, me // cols, :, pl.ds(my_col, LANE)]
            remote(piece, piece, ag_send.at[it], ag_recv.at[it], band, peer).start()

        to_members(send_piece)
        if it + 1 < ITERS:
            build_hot(it + 1)
        drain(band_sums.at[it], sc_recv.at[it, 0])
        total_sums[it] = sums[it] + jnp.sum(band_sums[it], axis=0)
        to_members(
            lambda k, peer: remote(
                total_sums.at[it], member_sums.at[it, k - 1], sc_send.at[it, 1], sc_recv.at[it, 1], band, peer
            ).start()
        )
        drain(member_sums.at[it], sc_recv.at[it, 1])
        total = jnp.sum(total_sums[it] + jnp.sum(member_sums[it], axis=0), axis=1, keepdims=True)
        step = (total[0:1] - total[1:2]) / (total[0:1] + total[2:3])
        steps.append(step)
        fields.append([step * d for d in pieces])
        drain(arrived.at[it], ag_recv.at[it])
        if it + 1 < ITERS:
            for r in range(lat // 8):
                a = r * 8 * levels
                hi, lo = split(direc[it, r])
                split_dir[a : a + 8 * levels, :] = hi.astype(BF16)
                split_dir[rows + a : rows + a + 8 * levels, :] = lo.astype(BF16)

    for level in range(levels):
        for r in range(lat // 8):
            a = level * 8
            out_ref[level, r * 8 : r * 8 + 8, :] = (
                steps[0] * direc[0, r, a : a + 8, :] + steps[1] * direc[1, r, a : a + 8, :]
            )

    drain(got_obs, obs_send.at[0])
    drain(got_obs, obs_send.at[1])
    for it in range(ITERS):
        for level in range(levels):
            drain(arrived.at[it, level], rs_send.at[it, level])
        drain(arrived.at[it], ag_send.at[it])
        drain(band_sums.at[it], sc_send.at[it, 0])
        drain(member_sums.at[it], sc_send.at[it, 1])


def local(n_band, n_member, ensemble, variance, obs_index, obs_value, obs_error, root_ranks):
    members_here, levels, lat, lon = ensemble.shape
    wide, mid, rows = lat + 2 * HALO, lat + 2 * HALF, levels * lat
    halves = members_here // QUAD
    rest = n_member - 1
    dma = pltpu.SemaphoreType.DMA
    vmem = pl.BlockSpec(memory_space=pltpu.VMEM)
    hbm = pl.BlockSpec(memory_space=pl.ANY)
    return pl.pallas_call(
        functools.partial(kernel, n_band, n_member, members_here, levels, lat, lon),
        out_shape=jax.ShapeDtypeStruct((levels, lat, lon), F32),
        in_specs=[pl.BlockSpec(memory_space=pltpu.SMEM), hbm, hbm, vmem, vmem, vmem],
        out_specs=vmem,
        scratch_shapes=[
            pltpu.VMEM((members_here, levels, wide, lon), BF16),
            pltpu.VMEM((2 * BLK, BLK), BF16),
            pltpu.VMEM((QUAD * mid, QUAD * wide), BF16),
            pltpu.VMEM((QUAD * lat, QUAD * mid), BF16),
            pltpu.VMEM((n_member, 8, LANE), F32),
            pltpu.VMEM((rest, 8, LANE), F32),
            pltpu.VMEM((n_member, 8, LANE), F32),
            pltpu.VMEM((n_member // GROUP, lon, GROUP * LANE), BF16),
            pltpu.VMEM((2 * rows, lon), F32),
            pltpu.VMEM((2 * 8 * levels, LANE), F32),
            pltpu.VMEM((ITERS, levels, wide, lon), F32),
            pltpu.VMEM((halves, QUAD * wide, lon + 2 * LANE), BF16),
            pltpu.VMEM((halves, QUAD * wide, lon), BF16),
            pltpu.VMEM((halves, QUAD * mid, lon + 2 * LANE), BF16),
            pltpu.VMEM((halves, QUAD * mid, lon), BF16),
            pltpu.VMEM((ITERS, levels, lat, lon), F32),
            pltpu.VMEM((ITERS, levels, rest, 8, LANE), F32),
            pltpu.VMEM((levels, 8, LANE), F32),
            pltpu.VMEM((ITERS, lat // 8, 8 * levels, lon), F32),
            pltpu.VMEM((2 * rows, lon), BF16),
            pltpu.VMEM((ITERS, 8, LANE), F32),
            pltpu.VMEM((ITERS, n_band - 1, 8, LANE), F32),
            pltpu.VMEM((ITERS, 8, LANE), F32),
            pltpu.VMEM((ITERS, rest, 8, LANE), F32),
            dma((2,)),
            dma((2,)), dma((2,)),
            dma((2,)), dma((2,)),
            dma((ITERS, 2)), dma((ITERS, 2)),
            dma((ITERS, levels)), dma((ITERS, levels)),
            dma((ITERS,)), dma((ITERS,)),
            dma((ITERS, 2)), dma((ITERS, 2)),
        ],
        compiler_params=pltpu.CompilerParams(
            collective_id=0, has_side_effects=True, vmem_limit_bytes=52 * 1024 * 1024
        ),
    )(root_ranks, ensemble, variance, obs_index, obs_value, obs_error)


def solution(mesh):
    in_specs = (
        P("member", None, "band", None),
        P(None, "band", None),
        P("member", "band"),
        P("member", "band"),
        P("member", "band"),
        P(),
    )
    body = functools.partial(local, mesh.shape["band"], mesh.shape["member"])
    return jax.shard_map(body, mesh=mesh, in_specs=in_specs, out_specs=P(None, "band", None), check_vma=False)
```

time: 533 us -> 125 us (0.23)
  blocking collectives: 197 us -> 0 us
  Pallas kernels: 0 us -> 119 us
  local copies, waits for them, and re-layouts: 103 us -> 4.64 us
  waiting for transfers between devices: 61.4 us -> 0 us
  starting transfers between devices: 59.6 us -> 0 us
  other arithmetic: 58.2 us -> 0 us
  matrix products: 36 us -> 0 us
  between operations: 12.8 us -> 0.01 us
    psum x10 -> x0, blocking collectives: 139 us -> none  [the longest x8 105 us: one_axis_at_a_time(): x = lax.psum(x, axis)]
    pallas_call x0 -> x1, Pallas kernels: none -> 119 us  [local(): pl.pallas_call(functools.partial(kernel, n_band, n_member, members_here,...]
    gather x4 -> x0, local copies, waits for them, and re-layouts: 92.1 us -> none  [the longest x2 46.1 us: make_gradient(): departure = values - field.reshape(-1)[positions]]
    ppermute x4 -> x0, starting transfers between devices: 44.4 us -> none  [the longest x2 40.4 us: with_halo(): before = lax.ppermute(last, axis, up)]
    scatter-add x2 -> x0, other arithmetic: 44.3 us -> none  [make_gradient(): flat = jnp.zeros((field.size,), jnp.float32).at[positions].add(weight * d...]
    all_gather x1 -> x0, blocking collectives: 41.4 us -> none  [picked(): lax.all_gather(x, axis)]
    dot_general x6 -> x0, matrix products: 36 us -> none  [the longest x4 24.9 us: apply_rows(): jnp.einsum('ij,bjk->bik', matrix, padded, preferred_element_type=jnp.floa...]
    all_to_all x3 -> x0, waiting for transfers between devices: 32.9 us -> none  [the longest x2 21.5 us: summed_on_arrival(): parts = lax.all_to_all(in_blocks(x, dim, count), axis, 0, 0, tiled=True)]
  transfers between devices with their start and end apart: 7 -> 0, of which waited for: 7 -> 0; matrix products, arithmetic and copies ran while one was open for 0% -> 0% of each run, Pallas kernels for 0% -> 0%
where the time goes in v1:
time: 125 us; the launch traced here: 124 us
  Pallas kernels  119 us (95%)
  local copies, waits for them, and re-layouts  4.64 us (4%)
    pallas_call x1, Pallas kernels, local(): pl.pallas_call(functools.partial(kernel, n_band, n_member, members_here,...  119 us
    unnamed x11, local copies, waits for them, and re-layouts  4.64 us

profile of v1, /device:TPU:1, one launch (start us, length us, event | category | flops | bytes accessed | tf_op | source)
XLA Modules:
  0.0 124.0 jit_solution(12173884965267663736)
XLA Ops:
  0.0 0.0 copy-start
  0.0 1.0 copy-done
  1.0 0.0 copy-start.1
  1.0 0.7 copy-done.1
  1.8 0.0 copy-start.2
  1.8 0.7 copy-done.2
  2.5 0.0 copy-start.3
  2.5 0.7 copy-done.3
  3.2 0.0 copy-start.4
  3.2 0.7 copy-done.4
  3.9 119.4 %shard_map.64 = f32[4,32,1024]{2,1,0:T(8,128)S(1)} custom-call(s32[2]{0:T(128)S(1)} %copy-done.4, bf16[8,4,32,1024]{3,2,1,0:T(8,128)(2,1)} %ens_ref.1, f32[4,32,1024]{2,1,0:T(8,128)S(1)} %copy-done, s32[1,4096]{1,0:T(1,128)S(1)} %copy-done.1, f32[1,4096]{1,0:T(1,128)S(1)} %copy-done.2, f32[1,4096]{1,0:T(1,128)S(1)} %copy-done.3), custom_call_target="tpu_custom_call" | custom-call | tf_op jit(solution)/shard_map/pallas_call | solution.py:368
  123.2 0.8 copy.8
Async XLA Ops:
  0.0 1.0 copy-start
  1.0 0.7 copy-start.1
  1.8 0.7 copy-start.2
  2.5 0.7 copy-start.3
  3.2 0.7 copy-start.4

commit v2 on v1

--- a/solution.py
+++ b/solution.py
@@ -44,12 +44,13 @@
 
 def kernel(
     n_band, n_member, members_here, levels, lat, lon,
-    root_ref, ens_ref, var_ref, idx_ref, val_ref, err_ref, out_ref,
-    ext, wlon, lat1, lat2, send_obs, got_obs, obs, hot, grad, grad2, gpad,
-    xpad, ypad, zpad, vpad, spread, arrived, varp, direc, split_dir,
+    root_hbm, ens_ref, var_ref, idx_hbm, val_hbm, err_hbm, out_ref,
+    root_ref, idx_ref, val_ref, err_ref,
+    ext, wlon, lat1, lat2, send_obs, got_obs, obs, hot, lhs, lhs2, reached, grad2, gpad,
+    xpad, ypad, zpad, vpad, spread, arrived, varp, direc, direc_lo,
     sums, band_sums, total_sums, member_sums,
     own_sem, ens_send, ens_recv, obs_send, obs_recv, halo_send, halo_recv,
-    rs_send, rs_recv, ag_send, ag_recv, sc_send, sc_recv,
+    rs_send, rs_recv, ag_send, ag_recv, lo_send, lo_recv, sc_send, sc_recv,
 ):
     me = lax.axis_index("member")
     band = lax.axis_index("band")
@@ -78,6 +79,15 @@
             return carry
         lax.fori_loop(1, n_member, body, 0)
 
+    loads = [
+        pltpu.make_async_copy(src, dst, own_sem.at[2 + i])
+        for i, (src, dst) in enumerate(
+            ((root_hbm, root_ref), (idx_hbm, idx_ref), (val_hbm, val_ref), (err_hbm, err_ref))
+        )
+    ]
+    for load in loads:
+        load.start()
+
     barrier = pltpu.get_barrier_semaphore()
 
     def greet_member(k, peer):
@@ -99,6 +109,9 @@
         var_ref.at[:, pl.ds(my_row, 8), pl.ds(my_col, LANE)], varp, own_sem.at[1]
     )
     own_var.start()
+
+    for load in loads:
+        load.wait()
 
     flags = [(root_ref[it] == me).astype(F32) for it in range(ITERS)]
     for j in range(n_member):
@@ -156,51 +169,81 @@
     def line(g, which):
         return jnp.concatenate([obs[g * GROUP + j, which : which + 1, :] for j in range(GROUP)], axis=1)
 
+    def columns(g):
+        return pl.ds(pl.multiple_of(g * width, width), width)
+
+    def each_group(step):
+        def body(g, carry):
+            step(g)
+            return carry
+        lax.fori_loop(0, groups, body, 0)
+
     def build_hot(it):
-        def body(g, carry):
+        def step(g):
             column = line(g, 3 * it).astype(jnp.int32) % lon
             for r in range(0, lon, LANE):
                 hit = iota((LANE, width), 0) + r == column
-                hot[g, r : r + LANE, :] = jnp.where(hit, 1.0, 0.0).astype(BF16)
-            return carry
-        lax.fori_loop(0, groups, body, 0)
+                hot[r : r + LANE, columns(g)] = jnp.where(hit, 1.0, 0.0).astype(BF16)
+        each_group(step)
 
     nt = (((1,), (1,)), ((), ()))
 
-    def build_gradient(it, step):
-        grad[...] = jnp.zeros_like(grad)
-        grad2[...] = jnp.zeros_like(grad2)
-
-        def body(g, carry):
-            place = line(g, 3 * it).astype(jnp.int32)
+    def gather(it):
+        field = direc[it - 1].reshape(rows, lon)
+
+        def step(g):
+            row = line(g, 3 * it).astype(jnp.int32) // lon
+            level, in_level = row // lat, row % lat
+            line_of = (in_level // 8) * (8 * levels) + level * 8 + in_level % 8
+            found = jnp.dot(field, hot[:, columns(g)], preferred_element_type=F32)
+            found = jnp.where(iota((rows, width), 0) == line_of, found, 0.0)
+            reached[:, columns(g)] = jnp.sum(found, axis=0, keepdims=True)
+        each_group(step)
+
+    def build_terms(it, scale):
+        def step(g):
             values = line(g, 3 * it + 1)
             errors = line(g, 3 * it + 2)
-            row = place // lon
+            row = line(g, 3 * it).astype(jnp.int32) // lon
             departure = values
             if it > 0:
-                level, in_level = row // lat, row % lat
-                line_of = (in_level // 8) * (8 * levels) + level * 8 + in_level % 8
-                found = jnp.dot(split_dir[...], hot[g], preferred_element_type=F32)
-                found = found[:rows] + found[rows:]
-                reached = jnp.sum(jnp.where(iota((rows, width), 0) == line_of, found, 0.0), axis=0, keepdims=True)
-                departure = values - step * reached
+                departure = values - scale * reached[:, columns(g)]
             weight = huber_edge / jnp.maximum(jnp.abs(departure / errors), huber_edge)
             square = errors * errors
             hit = iota((rows, width), 0) == row
-            terms = [jnp.where(hit, part, 0.0).astype(BF16) for part in split(weight * departure / square)]
-            grad[...] += lax.dot_general(jnp.concatenate(terms, axis=0), hot[g], nt, preferred_element_type=F32)
+            for i, part in enumerate(split(weight * departure / square)):
+                lhs[i * rows : (i + 1) * rows, columns(g)] = jnp.where(hit, part, 0.0).astype(BF16)
             mine = iota((8 * levels, width), 0)
             hit = (mine // 8) * lat + my_row + mine % 8 == row
-            terms = [jnp.where(hit, part, 0.0).astype(BF16) for part in split(weight / square)]
-            grad2[...] += lax.dot_general(
-                jnp.concatenate(terms, axis=0), hot[g, pl.ds(my_col, LANE), :], nt, preferred_element_type=F32
-            )
-            return carry
-
-        lax.fori_loop(0, groups, body, 0)
-        for level in range(levels):
-            a, b = level * lat, rows + level * lat
-            gpad[it, level, HALO : HALO + lat, :] = grad[a : a + lat, :] + grad[b : b + lat, :]
+            for i, part in enumerate(split(weight / square)):
+                a = i * 8 * levels
+                lhs2[a : a + 8 * levels, columns(g)] = jnp.where(hit, part, 0.0).astype(BF16)
+        each_group(step)
+
+    def halos(it, b):
+        at = pl.ds(b * BLK, BLK)
+        return [
+            remote(
+                gpad.at[it, :, pl.ds(lat, HALO), at], gpad.at[it, :, pl.ds(0, HALO), at],
+                halo_send.at[it, 0, b], halo_recv.at[it, 0, b], up, me,
+            ),
+            remote(
+                gpad.at[it, :, pl.ds(HALO, HALO), at], gpad.at[it, :, pl.ds(HALO + lat, HALO), at],
+                halo_send.at[it, 1, b], halo_recv.at[it, 1, b], down, me,
+            ),
+        ]
+
+    def scatter(it):
+        for b in range(lon // BLK):
+            at = slice(b * BLK, (b + 1) * BLK)
+            both = lax.dot_general(lhs[...], hot[at, :], nt, preferred_element_type=F32)
+            block = both[:rows] + both[rows:]
+            gpad[it, :, HALO : HALO + lat, at] = block.reshape(levels, lat, BLK)
+            for copy in halos(it, b):
+                copy.start()
+        grad2[...] = lax.dot_general(
+            lhs2[...], hot[pl.ds(my_col, LANE), :], nt, preferred_element_type=F32
+        )
 
     def lon_filter(padded, store):
         for c in range(0, lon, BLK):
@@ -214,22 +257,34 @@
         if at.stop == lon:
             ref[:, :LANE] = block[:, block.shape[1] - LANE :]
 
+    def lon_of_rows(it, level, at_rows):
+        for c in range(0, lon, BLK):
+            at = slice(c, c + BLK)
+            blocks = []
+            for part in at_rows:
+                mixed = ext[:, level, part, at].astype(F32) * gpad[it, level, part, at][None]
+                blocks.append(mixed.astype(BF16).reshape(members_here * (part.stop - part.start), BLK))
+            put_padded(xpad, at, jnp.concatenate(blocks, axis=0))
+
+        def store(at, block):
+            a = 0
+            for part in at_rows:
+                length = part.stop - part.start
+                size = members_here * length
+                ypad[level, :, part, at] = block[a : a + size].reshape(members_here, length, BLK)
+                a += size
+
+        lon_filter(xpad, store)
+
     def filters(it, level):
+        lon_of_rows(it, level, (slice(0, HALO), slice(HALO + lat, wide)))
         for h in range(members_here // QUAD):
             who = slice(h * QUAD, (h + 1) * QUAD)
-            xs, ys, zs, vs = xpad.at[h], ypad.at[h], zpad.at[h], vpad.at[h]
+            zs, vs = zpad.at[h], vpad.at[h]
             for c in range(0, lon, BLK):
                 at = slice(c, c + BLK)
-                mixed = ext[who, level, :, at].astype(F32) * gpad[it, level, :, at][None]
-                put_padded(xs, at, mixed.astype(BF16).reshape(QUAD * wide, BLK))
-
-            def store_y(at, block):
-                ys[:, at] = block
-
-            lon_filter(xs, store_y)
-            for c in range(0, lon, BLK):
-                at = slice(c, c + BLK)
-                put_padded(zs, at, jnp.dot(lat1[...], ys[:, at], preferred_element_type=F32).astype(BF16))
+                first = ypad[level, who, :, at].reshape(QUAD * wide, BLK)
+                put_padded(zs, at, jnp.dot(lat1[...], first, preferred_element_type=F32).astype(BF16))
 
             def store_v(at, block):
                 vs[:, at] = block
@@ -248,24 +303,23 @@
     fields = []
     build_hot(0)
     for it in range(ITERS):
-        build_gradient(it, steps[-1] if steps else None)
-        halo_up = remote(
-            gpad.at[it, :, pl.ds(lat, HALO), :], gpad.at[it, :, pl.ds(0, HALO), :],
-            halo_send.at[it, 0], halo_recv.at[it, 0], up, me,
-        )
-        halo_down = remote(
-            gpad.at[it, :, pl.ds(HALO, HALO), :], gpad.at[it, :, pl.ds(HALO + lat, HALO), :],
-            halo_send.at[it, 1], halo_recv.at[it, 1], down, me,
-        )
-        halo_up.start()
-        halo_down.start()
+        build_terms(it, steps[-1] if steps else None)
+        scatter(it)
         if it == 0:
             own.wait()
             own_var.wait()
+
+        def middle(level, carry):
+            lon_of_rows(it, level, (slice(HALO, HALO + lat),))
+            return carry
+
+        lax.fori_loop(0, levels, middle, 0)
+        if it == 0:
             ens_up.wait()
             ens_down.wait()
-        halo_up.wait()
-        halo_down.wait()
+        for b in range(lon // BLK):
+            for copy in halos(it, b):
+                copy.wait()
 
         def level_body(level, carry):
             filters(it, level)
@@ -298,7 +352,6 @@
             curve += c * d * d
             if it > 0:
                 back += fields[-1][level] * g
-            direc[it, me // cols, a : a + 8, pl.ds(my_col, LANE)] = d
             pieces.append(d)
         sums[it] = jnp.concatenate(
             [jnp.sum(x, axis=0, keepdims=True) for x in (along, back, curve)] + [jnp.zeros((5, LANE), F32)], axis=0
@@ -312,6 +365,9 @@
             return carry
 
         lax.fori_loop(1, n_band, send_sums, 0)
+
+        hi, lo = split(jnp.concatenate(pieces, axis=0))
+        direc[it, me // cols, :, pl.ds(my_col, LANE)] = hi.astype(BF16)
 
         def send_piece(k, peer):
             piece = direc.at[it, me // cols, :, pl.ds(my_col, LANE)]
@@ -327,34 +383,39 @@
                 total_sums.at[it], member_sums.at[it, k - 1], sc_send.at[it, 1], sc_recv.at[it, 1], band, peer
             ).start()
         )
+        drain(arrived.at[it, pl.ds(0, levels // 2)], ag_recv.at[it])
+        if it + 1 < ITERS:
+            gather(it + 1)
         drain(member_sums.at[it], sc_recv.at[it, 1])
         total = jnp.sum(total_sums[it] + jnp.sum(member_sums[it], axis=0), axis=1, keepdims=True)
         step = (total[0:1] - total[1:2]) / (total[0:1] + total[2:3])
         steps.append(step)
         fields.append([step * d for d in pieces])
-        drain(arrived.at[it], ag_recv.at[it])
         if it + 1 < ITERS:
-            for r in range(lat // 8):
-                a = r * 8 * levels
-                hi, lo = split(direc[it, r])
-                split_dir[a : a + 8 * levels, :] = hi.astype(BF16)
-                split_dir[rows + a : rows + a + 8 * levels, :] = lo.astype(BF16)
-
-    for level in range(levels):
-        for r in range(lat // 8):
-            a = level * 8
-            out_ref[level, r * 8 : r * 8 + 8, :] = (
-                steps[0] * direc[0, r, a : a + 8, :] + steps[1] * direc[1, r, a : a + 8, :]
-            )
+            direc_lo[me // cols, :, pl.ds(my_col, LANE)] = lo.astype(BF16)
+
+            def send_lo(k, peer):
+                piece = direc_lo.at[me // cols, :, pl.ds(my_col, LANE)]
+                remote(piece, piece, lo_send, lo_recv, band, peer).start()
+
+            to_members(send_lo)
+
+    drain(arrived.at[0, pl.ds(0, levels // 2)], lo_recv)
+    for r in range(lat // 8):
+        first = direc[0, r].astype(F32) + direc_lo[r].astype(F32)
+        moved = steps[0] * first + steps[1] * direc[1, r].astype(F32)
+        for level in range(levels):
+            out_ref[level, r * 8 : r * 8 + 8, :] = moved[level * 8 : level * 8 + 8]
 
     drain(got_obs, obs_send.at[0])
     drain(got_obs, obs_send.at[1])
     for it in range(ITERS):
         for level in range(levels):
             drain(arrived.at[it, level], rs_send.at[it, level])
-        drain(arrived.at[it], ag_send.at[it])
+        drain(arrived.at[it, pl.ds(0, levels // 2)], ag_send.at[it])
         drain(band_sums.at[it], sc_send.at[it, 0])
         drain(member_sums.at[it], sc_send.at[it, 1])
+    drain(arrived.at[0, pl.ds(0, levels // 2)], lo_send)
 
 
 def local(n_band, n_member, ensemble, variance, obs_index, obs_value, obs_error, root_ranks):
@@ -364,13 +425,17 @@
     rest = n_member - 1
     dma = pltpu.SemaphoreType.DMA
     vmem = pl.BlockSpec(memory_space=pltpu.VMEM)
-    hbm = pl.BlockSpec(memory_space=pl.ANY)
+    hbm = pl.BlockSpec(memory_space=pltpu.HBM)
     return pl.pallas_call(
         functools.partial(kernel, n_band, n_member, members_here, levels, lat, lon),
         out_shape=jax.ShapeDtypeStruct((levels, lat, lon), F32),
-        in_specs=[pl.BlockSpec(memory_space=pltpu.SMEM), hbm, hbm, vmem, vmem, vmem],
+        in_specs=[hbm] * 6,
         out_specs=vmem,
         scratch_shapes=[
+            pltpu.SMEM((ITERS,), jnp.int32),
+            pltpu.VMEM((1, n_member * LANE), jnp.int32),
+            pltpu.VMEM((1, n_member * LANE), F32),
+            pltpu.VMEM((1, n_member * LANE), F32),
             pltpu.VMEM((members_here, levels, wide, lon), BF16),
             pltpu.VMEM((2 * BLK, BLK), BF16),
             pltpu.VMEM((QUAD * mid, QUAD * wide), BF16),
@@ -378,33 +443,36 @@
             pltpu.VMEM((n_member, 8, LANE), F32),
             pltpu.VMEM((rest, 8, LANE), F32),
             pltpu.VMEM((n_member, 8, LANE), F32),
-            pltpu.VMEM((n_member // GROUP, lon, GROUP * LANE), BF16),
-            pltpu.VMEM((2 * rows, lon), F32),
+            pltpu.VMEM((lon, n_member * LANE), BF16),
+            pltpu.VMEM((2 * rows, n_member * LANE), BF16),
+            pltpu.VMEM((2 * 8 * levels, n_member * LANE), BF16),
+            pltpu.VMEM((1, n_member * LANE), F32),
             pltpu.VMEM((2 * 8 * levels, LANE), F32),
             pltpu.VMEM((ITERS, levels, wide, lon), F32),
-            pltpu.VMEM((halves, QUAD * wide, lon + 2 * LANE), BF16),
-            pltpu.VMEM((halves, QUAD * wide, lon), BF16),
+            pltpu.VMEM((members_here * lat, lon + 2 * LANE), BF16),
+            pltpu.VMEM((levels, members_here, wide, lon), BF16),
             pltpu.VMEM((halves, QUAD * mid, lon + 2 * LANE), BF16),
             pltpu.VMEM((halves, QUAD * mid, lon), BF16),
             pltpu.VMEM((ITERS, levels, lat, lon), F32),
             pltpu.VMEM((ITERS, levels, rest, 8, LANE), F32),
             pltpu.VMEM((levels, 8, LANE), F32),
-            pltpu.VMEM((ITERS, lat // 8, 8 * levels, lon), F32),
-            pltpu.VMEM((2 * rows, lon), BF16),
+            pltpu.VMEM((ITERS, lat // 8, 8 * levels, lon), BF16),
+            pltpu.VMEM((lat // 8, 8 * levels, lon), BF16),
             pltpu.VMEM((ITERS, 8, LANE), F32),
             pltpu.VMEM((ITERS, n_band - 1, 8, LANE), F32),
             pltpu.VMEM((ITERS, 8, LANE), F32),
             pltpu.VMEM((ITERS, rest, 8, LANE), F32),
-            dma((2,)),
+            dma((6,)),
             dma((2,)), dma((2,)),
             dma((2,)), dma((2,)),
-            dma((ITERS, 2)), dma((ITERS, 2)),
+            dma((ITERS, 2, lon // BLK)), dma((ITERS, 2, lon // BLK)),
             dma((ITERS, levels)), dma((ITERS, levels)),
             dma((ITERS,)), dma((ITERS,)),
+            dma, dma,
             dma((ITERS, 2)), dma((ITERS, 2)),
         ],
         compiler_params=pltpu.CompilerParams(
-            collective_id=0, has_side_effects=True, vmem_limit_bytes=52 * 1024 * 1024
+            collective_id=0, has_side_effects=True, vmem_limit_bytes=65500 * 1024
         ),
     )(root_ranks, ensemble, variance, obs_index, obs_value, obs_error)
 

time: 125 us -> 107 us (0.86)
  Pallas kernels: 119 us -> 105 us
  local copies, waits for them, and re-layouts: 4.64 us -> 1.89 us
    pallas_call x1, Pallas kernels: 119 us -> 105 us  [local(): pl.pallas_call(functools.partial(kernel, n_band, n_member, members_here,...]
    unnamed x11 -> x1, local copies, waits for them, and re-layouts: 4.64 us -> 1.89 us
where the time goes in v2:
time: 107 us
  Pallas kernels  105 us (98%)
  local copies, waits for them, and re-layouts  1.89 us (2%)
    pallas_call x1, Pallas kernels, local(): pl.pallas_call(functools.partial(kernel, n_band, n_member, members_here,...  105 us

profile of v2, /device:TPU:1, one launch (start us, length us, event | category | flops | bytes accessed | tf_op | source)
XLA Modules:
  0.0 106.9 jit_solution(263626702531870926)
XLA Ops:
  0.0 105.0 %shard_map.64 = f32[4,32,1024]{2,1,0:T(8,128)} custom-call(s32[2]{0:T(128)} %root_hbm.1, bf16[8,4,32,1024]{3,2,1,0:T(8,128)(2,1)} %ens_ref.1, f32[4,32,1024]{2,1,0:T(8,128)} %var_ref.1, s32[1,4096]{1,0:T(1,128)} %idx_hbm.1, f32[1,4096]{1,0:T(1,128)} %val_hbm.1, f32[1,4096]{1,0:T(1,128)} %err_hbm.1), custom_call_target="tpu_custom_call" | custom-call | tf_op jit(solution)/shard_map/pallas_call | solution.py:429
  105.0 1.9 %copy.8 = f32[4,32,1024]{2,1,0:T(8,128)} copy(f32[4,32,1024]{2,1,0:T(8,128)} %shard_map.64) | data formatting | bytes 1048576

commit v3 on v2

--- a/solution.py
+++ b/solution.py
@@ -47,10 +47,10 @@
     root_hbm, ens_ref, var_ref, idx_hbm, val_hbm, err_hbm, out_ref,
     root_ref, idx_ref, val_ref, err_ref,
     ext, wlon, lat1, lat2, send_obs, got_obs, obs, hot, lhs, lhs2, reached, grad2, gpad,
-    xpad, ypad, zpad, vpad, spread, arrived, varp, direc, direc_lo,
-    sums, band_sums, total_sums, member_sums,
+    xpad, ypad, zpad, vpad, spread, from_x, of_x, from_z, arrived, varp, direc, direc_lo,
+    sums, near_sums, total_sums, far_sums,
     own_sem, ens_send, ens_recv, obs_send, obs_recv, halo_send, halo_recv,
-    rs_send, rs_recv, ag_send, ag_recv, lo_send, lo_recv, sc_send, sc_recv,
+    x_send, x_recv, z_send, z_recv, rs_send, rs_recv, ag_send, ag_recv, lo_send, lo_recv, sc_send, sc_recv,
 ):
     me = lax.axis_index("member")
     band = lax.axis_index("band")
@@ -61,8 +61,12 @@
     rows = levels * lat
     up = lax.rem(band + 1, n_band)
     down = lax.rem(band + n_band - 1, n_band)
-    my_row = pl.multiple_of((me // cols) * 8, 8)
-    my_col = pl.multiple_of((me % cols) * LANE, LANE)
+    my_x, my_z = me // cols, me % cols
+    n_x, n_z, n_y = n_member // cols, cols, n_band // 2
+    my_y, core = band // 2, band % 2
+    my_row = pl.multiple_of(my_x * 8, 8)
+    my_col = pl.multiple_of(my_z * LANE, LANE)
+    last = levels - 1
 
     def remote(src, dst, send, recv, to_band, to_member):
         return pltpu.make_async_remote_copy(
@@ -73,11 +77,22 @@
     def drain(ref, sem):
         pltpu.make_async_copy(ref, ref, sem).wait()
 
+    def each(first, stop, start):
+        def body(k, carry):
+            start(k)
+            return carry
+        lax.fori_loop(first, stop, body, 0)
+
     def to_members(start):
-        def body(k, carry):
-            start(k, lax.rem(me + k, n_member))
-            return carry
-        lax.fori_loop(1, n_member, body, 0)
+        each(1, n_member, lambda k: start(k, lax.rem(me + k, n_member)))
+
+    def near(k):
+        index = lax.rem(core * n_z + my_z + k, 2 * n_z)
+        return my_y * 2 + index // n_z, my_x * n_z + index % n_z
+
+    def far(k):
+        index = lax.rem(my_x * n_y + my_y + k, n_x * n_y)
+        return (index % n_y) * 2 + core, (index // n_y) * n_z + my_z
 
     loads = [
         pltpu.make_async_copy(src, dst, own_sem.at[2 + i])
@@ -90,18 +105,21 @@
 
     barrier = pltpu.get_barrier_semaphore()
 
-    def greet_member(k, peer):
-        pl.semaphore_signal(barrier, inc=1, device_id=(band, peer), device_id_type=pl.DeviceIdType.MESH)
-
-    to_members(greet_member)
-
-    def greet_band(k, carry):
+    def greet(to_band, to_member):
         pl.semaphore_signal(
-            barrier, inc=1, device_id=(lax.rem(band + k, n_band), me), device_id_type=pl.DeviceIdType.MESH
+            barrier, inc=1, device_id=(to_band, to_member), device_id_type=pl.DeviceIdType.MESH
         )
-        return carry
-
-    lax.fori_loop(1, n_band, greet_band, 0)
+
+    to_members(lambda k, peer: greet(band, peer))
+    each(0, n_z, lambda k: greet(my_y * 2 + 1 - core, my_x * n_z + k))
+
+    def greet_plane(k):
+        greet(lax.rem(my_y + 1 + k // n_x, n_y) * 2 + core, (k % n_x) * n_z + my_z)
+
+    greeted = n_x * (n_y - 1)
+    each(0, greeted, greet_plane)
+    greet(lax.rem(band + n_band + 2 * core - 1, n_band), me)
+    greeted += n_member - 1 + n_z + 1
 
     own = pltpu.make_async_copy(ens_ref, ext.at[:, :, pl.ds(HALO, lat), :], own_sem.at[0])
     own.start()
@@ -120,7 +138,7 @@
         lines = [part * flags[it] for it in range(ITERS) for part in parts]
         send_obs[j] = jnp.concatenate(lines + [jnp.zeros((2, LANE), F32)], axis=0)
 
-    pl.semaphore_wait(barrier, n_member - 1 + n_band - 1)
+    pl.semaphore_wait(barrier, greeted)
 
     to_members(
         lambda k, peer: remote(
@@ -324,26 +342,60 @@
         def level_body(level, carry):
             filters(it, level)
 
-            def send(k, peer):
-                row = pl.multiple_of((peer // cols) * 8, 8)
-                col = pl.multiple_of((peer % cols) * LANE, LANE)
+            @pl.when(level < last)
+            def _():
+                def send_x(k):
+                    to_x = lax.rem(my_x + k, n_x)
+                    row = pl.multiple_of(to_x * 8, 8)
+                    remote(
+                        spread.at[it, level, pl.ds(row, 8), :], from_x.at[it, level, k - 1],
+                        x_send.at[it, level], x_recv.at[it, level], band, to_x * n_z + my_z,
+                    ).start()
+
+                each(1, n_x, send_x)
+
+            @pl.when(level == last)
+            def _():
+                def send(k, peer):
+                    row = pl.multiple_of((peer // n_z) * 8, 8)
+                    col = pl.multiple_of((peer % n_z) * LANE, LANE)
+                    remote(
+                        spread.at[it, last, pl.ds(row, 8), pl.ds(col, LANE)], arrived.at[it, k - 1],
+                        rs_send.at[it], rs_recv.at[it], band, peer,
+                    ).start()
+
+                to_members(send)
+            return carry
+
+        lax.fori_loop(0, levels, level_body, 0)
+
+        def pass_on(level):
+            drain(from_x.at[it, level], x_recv.at[it, level])
+            of_x[it, level] = spread[it, level, pl.ds(my_row, 8), :] + jnp.sum(from_x[it, level], axis=0)
+
+            def send_z(k):
+                to_z = lax.rem(my_z + k, n_z)
+                col = pl.multiple_of(to_z * LANE, LANE)
                 remote(
-                    spread.at[it, level, pl.ds(row, 8), pl.ds(col, LANE)], arrived.at[it, level, k - 1],
-                    rs_send.at[it, level], rs_recv.at[it, level], band, peer,
+                    of_x.at[it, level, :, pl.ds(col, LANE)], from_z.at[it, level, k - 1],
+                    z_send.at[it, level], z_recv.at[it, level], band, my_x * n_z + to_z,
                 ).start()
 
-            to_members(send)
-            return carry
-
-        lax.fori_loop(0, levels, level_body, 0)
+            each(1, n_z, send_z)
+
+        each(0, last, pass_on)
 
         along = jnp.zeros((8, LANE), F32)
         back = jnp.zeros((8, LANE), F32)
         curve = jnp.zeros((8, LANE), F32)
         pieces = []
         for level in range(levels):
-            drain(arrived.at[it, level], rs_recv.at[it, level])
-            summed = spread[it, level, pl.ds(my_row, 8), pl.ds(my_col, LANE)] + jnp.sum(arrived[it, level], axis=0)
+            if level < last:
+                drain(from_z.at[it, level], z_recv.at[it, level])
+                summed = of_x[it, level, :, pl.ds(my_col, LANE)] + jnp.sum(from_z[it, level], axis=0)
+            else:
+                drain(arrived.at[it], rs_recv.at[it])
+                summed = spread[it, level, pl.ds(my_row, 8), pl.ds(my_col, LANE)] + jnp.sum(arrived[it], axis=0)
             g = gpad[it, level, pl.ds(HALO + my_row, 8), pl.ds(my_col, LANE)]
             d = ensemble_share * summed / (members_here * n_member - 1) + static_share * varp[level] * g
             a = level * 8
@@ -357,50 +409,45 @@
             [jnp.sum(x, axis=0, keepdims=True) for x in (along, back, curve)] + [jnp.zeros((5, LANE), F32)], axis=0
         )
 
-        def send_sums(k, carry):
-            remote(
-                sums.at[it], band_sums.at[it, k - 1], sc_send.at[it, 0], sc_recv.at[it, 0],
-                lax.rem(band + k, n_band), me,
-            ).start()
-            return carry
-
-        lax.fori_loop(1, n_band, send_sums, 0)
-
+        def send_sums(k):
+            remote(sums.at[it], near_sums.at[it, k - 1], sc_send.at[it, 0], sc_recv.at[it, 0], *near(k)).start()
+
+        each(1, 2 * n_z, send_sums)
         hi, lo = split(jnp.concatenate(pieces, axis=0))
-        direc[it, me // cols, :, pl.ds(my_col, LANE)] = hi.astype(BF16)
+        direc[it, my_x, :, pl.ds(my_col, LANE)] = hi.astype(BF16)
 
         def send_piece(k, peer):
-            piece = direc.at[it, me // cols, :, pl.ds(my_col, LANE)]
+            piece = direc.at[it, my_x, :, pl.ds(my_col, LANE)]
             remote(piece, piece, ag_send.at[it], ag_recv.at[it], band, peer).start()
 
         to_members(send_piece)
         if it + 1 < ITERS:
             build_hot(it + 1)
-        drain(band_sums.at[it], sc_recv.at[it, 0])
-        total_sums[it] = sums[it] + jnp.sum(band_sums[it], axis=0)
-        to_members(
-            lambda k, peer: remote(
-                total_sums.at[it], member_sums.at[it, k - 1], sc_send.at[it, 1], sc_recv.at[it, 1], band, peer
-            ).start()
-        )
-        drain(arrived.at[it, pl.ds(0, levels // 2)], ag_recv.at[it])
+        drain(near_sums.at[it], sc_recv.at[it, 0])
+        total_sums[it] = sums[it] + jnp.sum(near_sums[it], axis=0)
+
+        def send_total(k):
+            remote(total_sums.at[it], far_sums.at[it, k - 1], sc_send.at[it, 1], sc_recv.at[it, 1], *far(k)).start()
+
+        each(1, n_x * n_y, send_total)
+        drain(arrived, ag_recv.at[it])
         if it + 1 < ITERS:
             gather(it + 1)
-        drain(member_sums.at[it], sc_recv.at[it, 1])
-        total = jnp.sum(total_sums[it] + jnp.sum(member_sums[it], axis=0), axis=1, keepdims=True)
+        drain(far_sums.at[it], sc_recv.at[it, 1])
+        total = jnp.sum(total_sums[it] + jnp.sum(far_sums[it], axis=0), axis=1, keepdims=True)
         step = (total[0:1] - total[1:2]) / (total[0:1] + total[2:3])
         steps.append(step)
         fields.append([step * d for d in pieces])
         if it + 1 < ITERS:
-            direc_lo[me // cols, :, pl.ds(my_col, LANE)] = lo.astype(BF16)
+            direc_lo[my_x, :, pl.ds(my_col, LANE)] = lo.astype(BF16)
 
             def send_lo(k, peer):
-                piece = direc_lo.at[me // cols, :, pl.ds(my_col, LANE)]
+                piece = direc_lo.at[my_x, :, pl.ds(my_col, LANE)]
                 remote(piece, piece, lo_send, lo_recv, band, peer).start()
 
             to_members(send_lo)
 
-    drain(arrived.at[0, pl.ds(0, levels // 2)], lo_recv)
+    drain(arrived, lo_recv)
     for r in range(lat // 8):
         first = direc[0, r].astype(F32) + direc_lo[r].astype(F32)
         moved = steps[0] * first + steps[1] * direc[1, r].astype(F32)
@@ -410,12 +457,14 @@
     drain(got_obs, obs_send.at[0])
     drain(got_obs, obs_send.at[1])
     for it in range(ITERS):
-        for level in range(levels):
-            drain(arrived.at[it, level], rs_send.at[it, level])
-        drain(arrived.at[it, pl.ds(0, levels // 2)], ag_send.at[it])
-        drain(band_sums.at[it], sc_send.at[it, 0])
-        drain(member_sums.at[it], sc_send.at[it, 1])
-    drain(arrived.at[0, pl.ds(0, levels // 2)], lo_send)
+        for level in range(last):
+            drain(from_x.at[it, level], x_send.at[it, level])
+            drain(from_z.at[it, level], z_send.at[it, level])
+        drain(arrived.at[it], rs_send.at[it])
+        drain(arrived, ag_send.at[it])
+        drain(near_sums.at[it], sc_send.at[it, 0])
+        drain(far_sums.at[it], sc_send.at[it, 1])
+    drain(arrived, lo_send)
 
 
 def local(n_band, n_member, ensemble, variance, obs_index, obs_value, obs_error, root_ranks):
@@ -454,19 +503,24 @@
             pltpu.VMEM((halves, QUAD * mid, lon + 2 * LANE), BF16),
             pltpu.VMEM((halves, QUAD * mid, lon), BF16),
             pltpu.VMEM((ITERS, levels, lat, lon), F32),
-            pltpu.VMEM((ITERS, levels, rest, 8, LANE), F32),
+            pltpu.VMEM((ITERS, levels - 1, lat // 8 - 1, 8, lon), F32),
+            pltpu.VMEM((ITERS, levels - 1, 8, lon), F32),
+            pltpu.VMEM((ITERS, levels - 1, lon // LANE - 1, 8, LANE), F32),
+            pltpu.VMEM((ITERS, rest, 8, LANE), F32),
             pltpu.VMEM((levels, 8, LANE), F32),
             pltpu.VMEM((ITERS, lat // 8, 8 * levels, lon), BF16),
             pltpu.VMEM((lat // 8, 8 * levels, lon), BF16),
             pltpu.VMEM((ITERS, 8, LANE), F32),
-            pltpu.VMEM((ITERS, n_band - 1, 8, LANE), F32),
+            pltpu.VMEM((ITERS, 2 * (lon // LANE) - 1, 8, LANE), F32),
             pltpu.VMEM((ITERS, 8, LANE), F32),
-            pltpu.VMEM((ITERS, rest, 8, LANE), F32),
+            pltpu.VMEM((ITERS, (lat // 8) * (n_band // 2) - 1, 8, LANE), F32),
             dma((6,)),
             dma((2,)), dma((2,)),
             dma((2,)), dma((2,)),
             dma((ITERS, 2, lon // BLK)), dma((ITERS, 2, lon // BLK)),
-            dma((ITERS, levels)), dma((ITERS, levels)),
+            dma((ITERS, levels - 1)), dma((ITERS, levels - 1)),
+            dma((ITERS, levels - 1)), dma((ITERS, levels - 1)),
+            dma((ITERS,)), dma((ITERS,)),
             dma((ITERS,)), dma((ITERS,)),
             dma, dma,
             dma((ITERS, 2)), dma((ITERS, 2)),

time: 107 us -> 102 us (0.953)
  Pallas kernels: 105 us -> 100 us
    pallas_call x1, Pallas kernels: 105 us -> 100 us  [local(): pl.pallas_call(functools.partial(kernel, n_band, n_member, members_here,...]
where the time goes in v3:
time: 102 us
  Pallas kernels  100 us (98%)
  local copies, waits for them, and re-layouts  1.89 us (2%)
    pallas_call x1, Pallas kernels, local(): pl.pallas_call(functools.partial(kernel, n_band, n_member, members_here,...  100 us

profile of v3, /device:TPU:1, one launch (start us, length us, event | category | flops | bytes accessed | tf_op | source)
XLA Modules:
  0.0 102.1 jit_solution(12348319528788161599)
XLA Ops:
  0.0 100.2 %shard_map.64 = f32[4,32,1024]{2,1,0:T(8,128)} custom-call(s32[2]{0:T(128)} %root_hbm.1, bf16[8,4,32,1024]{3,2,1,0:T(8,128)(2,1)} %ens_ref.1, f32[4,32,1024]{2,1,0:T(8,128)} %var_ref.1, s32[1,4096]{1,0:T(1,128)} %idx_hbm.1, f32[1,4096]{1,0:T(1,128)} %val_hbm.1, f32[1,4096]{1,0:T(1,128)} %err_hbm.1), custom_call_target="tpu_custom_call" | custom-call | tf_op jit(solution)/shard_map/pallas_call | solution.py:478
  100.2 1.9 %copy.8 = f32[4,32,1024]{2,1,0:T(8,128)} copy(f32[4,32,1024]{2,1,0:T(8,128)} %shard_map.64) | data formatting | bytes 1048576

commit v4 on v3

--- a/solution.py
+++ b/solution.py
@@ -46,10 +46,10 @@
     n_band, n_member, members_here, levels, lat, lon,
     root_hbm, ens_ref, var_ref, idx_hbm, val_hbm, err_hbm, out_ref,
     root_ref, idx_ref, val_ref, err_ref,
-    ext, wlon, lat1, lat2, send_obs, got_obs, obs, hot, lhs, lhs2, reached, grad2, gpad,
+    ext, wlon, lat1, lat2, send_obs, got_obs, obs, hot, lhs, lhs2, reached, grad2, gpad, edges, halo,
     xpad, ypad, zpad, vpad, spread, from_x, of_x, from_z, arrived, varp, direc, direc_lo,
     sums, near_sums, total_sums, far_sums,
-    own_sem, ens_send, ens_recv, obs_send, obs_recv, halo_send, halo_recv,
+    own_sem, ens_send, ens_recv, obs_send, obs_recv, group_recv, halo_send, halo_recv,
     x_send, x_recv, z_send, z_recv, rs_send, rs_recv, ag_send, ag_recv, lo_send, lo_recv, sc_send, sc_recv,
 ):
     me = lax.axis_index("member")
@@ -176,10 +176,9 @@
     obs[me] = send_obs[me] + jnp.sum(got_obs[...], axis=0)
     to_members(
         lambda k, peer: remote(
-            obs.at[me], obs.at[me], obs_send.at[1], obs_recv.at[1], band, peer
+            obs.at[me], obs.at[me], obs_send.at[1], group_recv.at[me // GROUP], band, peer
         ).start()
     )
-    drain(got_obs, obs_recv.at[1])
 
     groups = n_member // GROUP
     width = GROUP * LANE
@@ -196,13 +195,11 @@
             return carry
         lax.fori_loop(0, groups, body, 0)
 
-    def build_hot(it):
-        def step(g):
-            column = line(g, 3 * it).astype(jnp.int32) % lon
-            for r in range(0, lon, LANE):
-                hit = iota((LANE, width), 0) + r == column
-                hot[r : r + LANE, columns(g)] = jnp.where(hit, 1.0, 0.0).astype(BF16)
-        each_group(step)
+    def hot_of(it, g):
+        column = line(g, 3 * it).astype(jnp.int32) % lon
+        for r in range(0, lon, LANE):
+            hit = iota((LANE, width), 0) + r == column
+            hot[r : r + LANE, columns(g)] = jnp.where(hit, 1.0, 0.0).astype(BF16)
 
     nt = (((1,), (1,)), ((), ()))
 
@@ -218,37 +215,32 @@
             reached[:, columns(g)] = jnp.sum(found, axis=0, keepdims=True)
         each_group(step)
 
-    def build_terms(it, scale):
-        def step(g):
-            values = line(g, 3 * it + 1)
-            errors = line(g, 3 * it + 2)
-            row = line(g, 3 * it).astype(jnp.int32) // lon
-            departure = values
-            if it > 0:
-                departure = values - scale * reached[:, columns(g)]
-            weight = huber_edge / jnp.maximum(jnp.abs(departure / errors), huber_edge)
-            square = errors * errors
-            hit = iota((rows, width), 0) == row
-            for i, part in enumerate(split(weight * departure / square)):
-                lhs[i * rows : (i + 1) * rows, columns(g)] = jnp.where(hit, part, 0.0).astype(BF16)
-            mine = iota((8 * levels, width), 0)
-            hit = (mine // 8) * lat + my_row + mine % 8 == row
-            for i, part in enumerate(split(weight / square)):
-                a = i * 8 * levels
-                lhs2[a : a + 8 * levels, columns(g)] = jnp.where(hit, part, 0.0).astype(BF16)
-        each_group(step)
+    def terms_of(it, scale, g):
+        values = line(g, 3 * it + 1)
+        errors = line(g, 3 * it + 2)
+        row = line(g, 3 * it).astype(jnp.int32) // lon
+        departure = values
+        if it > 0:
+            departure = values - scale * reached[:, columns(g)]
+        weight = huber_edge / jnp.maximum(jnp.abs(departure / errors), huber_edge)
+        square = errors * errors
+        hit = iota((rows, width), 0) == row
+        for i, part in enumerate(split(weight * departure / square)):
+            lhs[i * rows : (i + 1) * rows, columns(g)] = jnp.where(hit, part, 0.0).astype(BF16)
+        mine = iota((8 * levels, width), 0)
+        hit = (mine // 8) * lat + my_row + mine % 8 == row
+        for i, part in enumerate(split(weight / square)):
+            a = i * 8 * levels
+            lhs2[a : a + 8 * levels, columns(g)] = jnp.where(hit, part, 0.0).astype(BF16)
 
     def halos(it, b):
         at = pl.ds(b * BLK, BLK)
         return [
             remote(
-                gpad.at[it, :, pl.ds(lat, HALO), at], gpad.at[it, :, pl.ds(0, HALO), at],
-                halo_send.at[it, 0, b], halo_recv.at[it, 0, b], up, me,
-            ),
-            remote(
-                gpad.at[it, :, pl.ds(HALO, HALO), at], gpad.at[it, :, pl.ds(HALO + lat, HALO), at],
-                halo_send.at[it, 1, b], halo_recv.at[it, 1, b], down, me,
-            ),
+                edges.at[it, :, pl.ds((1 - side) * (lat - HALO), HALO), at], halo.at[it, side, :, :, at],
+                halo_send.at[it, side, b], halo_recv.at[it, side, b], to, me,
+            )
+            for side, to in enumerate((up, down))
         ]
 
     def scatter(it):
@@ -256,7 +248,8 @@
             at = slice(b * BLK, (b + 1) * BLK)
             both = lax.dot_general(lhs[...], hot[at, :], nt, preferred_element_type=F32)
             block = both[:rows] + both[rows:]
-            gpad[it, :, HALO : HALO + lat, at] = block.reshape(levels, lat, BLK)
+            edges[it, :, :, at] = block.reshape(levels, lat, BLK).astype(BF16)
+            gpad[it, :, :, at] = block.reshape(levels, lat, BLK)
             for copy in halos(it, b):
                 copy.start()
         grad2[...] = lax.dot_general(
@@ -275,12 +268,12 @@
         if at.stop == lon:
             ref[:, :LANE] = block[:, block.shape[1] - LANE :]
 
-    def lon_of_rows(it, level, at_rows):
+    def lon_of_rows(it, level, at_rows, gradients):
         for c in range(0, lon, BLK):
             at = slice(c, c + BLK)
             blocks = []
-            for part in at_rows:
-                mixed = ext[:, level, part, at].astype(F32) * gpad[it, level, part, at][None]
+            for part, gradient in zip(at_rows, gradients):
+                mixed = ext[:, level, part, at].astype(F32) * gradient[:, at].astype(F32)[None]
                 blocks.append(mixed.astype(BF16).reshape(members_here * (part.stop - part.start), BLK))
             put_padded(xpad, at, jnp.concatenate(blocks, axis=0))
 
@@ -295,7 +288,9 @@
         lon_filter(xpad, store)
 
     def filters(it, level):
-        lon_of_rows(it, level, (slice(0, HALO), slice(HALO + lat, wide)))
+        lon_of_rows(
+            it, level, (slice(0, HALO), slice(HALO + lat, wide)), (halo.at[it, 0, level], halo.at[it, 1, level])
+        )
         for h in range(members_here // QUAD):
             who = slice(h * QUAD, (h + 1) * QUAD)
             zs, vs = zpad.at[h], vpad.at[h]
@@ -319,16 +314,28 @@
 
     steps = []
     fields = []
-    build_hot(0)
+    my_group = me // GROUP
+    for g, size in ((0, GROUP - 1), (None, GROUP)):
+        def arrive(k):
+            at = lax.rem(my_group + k, groups)
+            drain(got_obs.at[pl.ds(0, size)], group_recv.at[at])
+            hot_of(0, at)
+            terms_of(0, None, at)
+
+        if g == 0:
+            arrive(0)
+        else:
+            each(1, groups, arrive)
     for it in range(ITERS):
-        build_terms(it, steps[-1] if steps else None)
+        if it > 0:
+            each_group(functools.partial(terms_of, it, steps[-1]))
         scatter(it)
         if it == 0:
             own.wait()
             own_var.wait()
 
         def middle(level, carry):
-            lon_of_rows(it, level, (slice(HALO, HALO + lat),))
+            lon_of_rows(it, level, (slice(HALO, HALO + lat),), (gpad.at[it, level],))
             return carry
 
         lax.fori_loop(0, levels, middle, 0)
@@ -396,7 +403,7 @@
             else:
                 drain(arrived.at[it], rs_recv.at[it])
                 summed = spread[it, level, pl.ds(my_row, 8), pl.ds(my_col, LANE)] + jnp.sum(arrived[it], axis=0)
-            g = gpad[it, level, pl.ds(HALO + my_row, 8), pl.ds(my_col, LANE)]
+            g = gpad[it, level, pl.ds(my_row, 8), pl.ds(my_col, LANE)]
             d = ensemble_share * summed / (members_here * n_member - 1) + static_share * varp[level] * g
             a = level * 8
             c = grad2[a : a + 8, :] + grad2[a + 8 * levels : a + 8 * levels + 8, :]
@@ -422,7 +429,7 @@
 
         to_members(send_piece)
         if it + 1 < ITERS:
-            build_hot(it + 1)
+            each_group(functools.partial(hot_of, it + 1))
         drain(near_sums.at[it], sc_recv.at[it, 0])
         total_sums[it] = sums[it] + jnp.sum(near_sums[it], axis=0)
 
@@ -497,7 +504,9 @@
             pltpu.VMEM((2 * 8 * levels, n_member * LANE), BF16),
             pltpu.VMEM((1, n_member * LANE), F32),
             pltpu.VMEM((2 * 8 * levels, LANE), F32),
-            pltpu.VMEM((ITERS, levels, wide, lon), F32),
+            pltpu.VMEM((ITERS, levels, lat, lon), F32),
+            pltpu.VMEM((ITERS, levels, lat, lon), BF16),
+            pltpu.VMEM((ITERS, 2, levels, HALO, lon), BF16),
             pltpu.VMEM((members_here * lat, lon + 2 * LANE), BF16),
             pltpu.VMEM((levels, members_here, wide, lon), BF16),
             pltpu.VMEM((halves, QUAD * mid, lon + 2 * LANE), BF16),
@@ -516,7 +525,7 @@
             pltpu.VMEM((ITERS, (lat // 8) * (n_band // 2) - 1, 8, LANE), F32),
             dma((6,)),
             dma((2,)), dma((2,)),
-            dma((2,)), dma((2,)),
+            dma((2,)), dma((1,)), dma((n_member // GROUP,)),
             dma((ITERS, 2, lon // BLK)), dma((ITERS, 2, lon // BLK)),
             dma((ITERS, levels - 1)), dma((ITERS, levels - 1)),
             dma((ITERS, levels - 1)), dma((ITERS, levels - 1)),

time: 102 us -> 101 us (level)
    pallas_call x1, Pallas kernels: 100 us -> 99.1 us  [local(): pl.pallas_call(functools.partial(kernel, n_band, n_member, members_here,...]
where the time goes in v4:
time: 101 us
  Pallas kernels  99.1 us (98%)
  local copies, waits for them, and re-layouts  1.89 us (2%)
    pallas_call x1, Pallas kernels, local(): pl.pallas_call(functools.partial(kernel, n_band, n_member, members_here,...  99.1 us

profile of v4, /device:TPU:1, one launch (start us, length us, event | category | flops | bytes accessed | tf_op | source)
XLA Modules:
  0.0 101.0 jit_solution(6121348292411408162)
XLA Ops:
  0.0 99.1 %shard_map.64 = f32[4,32,1024]{2,1,0:T(8,128)} custom-call(s32[2]{0:T(128)} %root_hbm.1, bf16[8,4,32,1024]{3,2,1,0:T(8,128)(2,1)} %ens_ref.1, f32[4,32,1024]{2,1,0:T(8,128)} %var_ref.1, s32[1,4096]{1,0:T(1,128)} %idx_hbm.1, f32[1,4096]{1,0:T(1,128)} %val_hbm.1, f32[1,4096]{1,0:T(1,128)} %err_hbm.1), custom_call_target="tpu_custom_call" | custom-call | tf_op jit(solution)/shard_map/pallas_call | solution.py:485
  99.1 1.9 %copy.8 = f32[4,32,1024]{2,1,0:T(8,128)} copy(f32[4,32,1024]{2,1,0:T(8,128)} %shard_map.64) | data formatting | bytes 1048576

commit v5 on v4

--- a/solution.py
+++ b/solution.py
@@ -437,6 +437,10 @@
             remote(total_sums.at[it], far_sums.at[it, k - 1], sc_send.at[it, 1], sc_recv.at[it, 1], *far(k)).start()
 
         each(1, n_x * n_y, send_total)
+        if it + 1 == ITERS:
+            drain(arrived, lo_recv)
+            for r in range(lat // 8):
+                out_ref[r] = steps[0] * (direc[0, r].astype(F32) + direc_lo[r].astype(F32))
         drain(arrived, ag_recv.at[it])
         if it + 1 < ITERS:
             gather(it + 1)
@@ -454,12 +458,8 @@
 
             to_members(send_lo)
 
-    drain(arrived, lo_recv)
     for r in range(lat // 8):
-        first = direc[0, r].astype(F32) + direc_lo[r].astype(F32)
-        moved = steps[0] * first + steps[1] * direc[1, r].astype(F32)
-        for level in range(levels):
-            out_ref[level, r * 8 : r * 8 + 8, :] = moved[level * 8 : level * 8 + 8]
+        out_ref[r] += steps[1] * direc[1, r].astype(F32)
 
     drain(got_obs, obs_send.at[0])
     drain(got_obs, obs_send.at[1])
@@ -482,9 +482,9 @@
     dma = pltpu.SemaphoreType.DMA
     vmem = pl.BlockSpec(memory_space=pltpu.VMEM)
     hbm = pl.BlockSpec(memory_space=pltpu.HBM)
-    return pl.pallas_call(
+    out = pl.pallas_call(
         functools.partial(kernel, n_band, n_member, members_here, levels, lat, lon),
-        out_shape=jax.ShapeDtypeStruct((levels, lat, lon), F32),
+        out_shape=jax.ShapeDtypeStruct((lat // 8, 8 * levels, lon), F32),
         in_specs=[hbm] * 6,
         out_specs=vmem,
         scratch_shapes=[
@@ -538,6 +538,7 @@
             collective_id=0, has_side_effects=True, vmem_limit_bytes=65500 * 1024
         ),
     )(root_ranks, ensemble, variance, obs_index, obs_value, obs_error)
+    return jnp.swapaxes(out.reshape(lat // 8, levels, 8, lon), 0, 1).reshape(levels, lat, lon)
 
 
 def solution(mesh):

time: 101 us -> 101 us (level)
    reshape x0 -> x1, local copies, waits for them, and re-layouts: none -> 1.89 us  [local(): jnp.swapaxes(out.reshape(lat // 8, levels, 8, lon), 0, 1)]
    unnamed x1 -> x0, local copies, waits for them, and re-layouts: 1.89 us -> none
where the time goes in v5:
time: 101 us
  Pallas kernels  99 us (98%)
  local copies, waits for them, and re-layouts  1.89 us (2%)
    pallas_call x1, Pallas kernels, local(): pl.pallas_call(functools.partial(kernel, n_band, n_member, members_here,...  99 us

profile of v5, /device:TPU:1, one launch (start us, length us, event | category | flops | bytes accessed | tf_op | source)
XLA Modules:
  0.0 100.9 jit_solution(640200073954642227)
XLA Ops:
  0.0 99.0 %shard_map.64 = f32[4,32,1024]{2,1,0:T(8,128)} custom-call(s32[2]{0:T(128)} %root_hbm.1, bf16[8,4,32,1024]{3,2,1,0:T(8,128)(2,1)} %ens_ref.1, f32[4,32,1024]{2,1,0:T(8,128)} %var_ref.1, s32[1,4096]{1,0:T(1,128)} %idx_hbm.1, f32[1,4096]{1,0:T(1,128)} %val_hbm.1, f32[1,4096]{1,0:T(1,128)} %err_hbm.1), custom_call_target="tpu_custom_call" | custom-call | tf_op jit(solution)/shard_map/pallas_call | solution.py:485
  99.0 1.9 %copy_bitcast_fusion = f32[4,32,1024]{2,1,0:T(8,128)} fusion(f32[4,32,1024]{2,1,0:T(8,128)} %shard_map.64), kind=kLoop, calls=%fused_computation | loop fusion | bytes 1048576 | tf_op jit(solution)/shard_map/reshape | solution.py:541

commit v6 on v4

--- a/solution.py
+++ b/solution.py
@@ -405,13 +405,24 @@
                 summed = spread[it, level, pl.ds(my_row, 8), pl.ds(my_col, LANE)] + jnp.sum(arrived[it], axis=0)
             g = gpad[it, level, pl.ds(my_row, 8), pl.ds(my_col, LANE)]
             d = ensemble_share * summed / (members_here * n_member - 1) + static_share * varp[level] * g
+            pieces.append(d)
+        hi, lo = split(jnp.concatenate(pieces, axis=0))
+        direc[it, my_x, :, pl.ds(my_col, LANE)] = hi.astype(BF16)
+
+        def send_piece(k, peer):
+            piece = direc.at[it, my_x, :, pl.ds(my_col, LANE)]
+            remote(piece, piece, ag_send.at[it], ag_recv.at[it], band, peer).start()
+
+        if it == 0:
+            to_members(send_piece)
+        for level, d in enumerate(pieces):
+            g = gpad[it, level, pl.ds(my_row, 8), pl.ds(my_col, LANE)]
             a = level * 8
             c = grad2[a : a + 8, :] + grad2[a + 8 * levels : a + 8 * levels + 8, :]
             along += g * d
             curve += c * d * d
             if it > 0:
                 back += fields[-1][level] * g
-            pieces.append(d)
         sums[it] = jnp.concatenate(
             [jnp.sum(x, axis=0, keepdims=True) for x in (along, back, curve)] + [jnp.zeros((5, LANE), F32)], axis=0
         )
@@ -420,14 +431,8 @@
             remote(sums.at[it], near_sums.at[it, k - 1], sc_send.at[it, 0], sc_recv.at[it, 0], *near(k)).start()
 
         each(1, 2 * n_z, send_sums)
-        hi, lo = split(jnp.concatenate(pieces, axis=0))
-        direc[it, my_x, :, pl.ds(my_col, LANE)] = hi.astype(BF16)
-
-        def send_piece(k, peer):
-            piece = direc.at[it, my_x, :, pl.ds(my_col, LANE)]
-            remote(piece, piece, ag_send.at[it], ag_recv.at[it], band, peer).start()
-
-        to_members(send_piece)
+        if it > 0:
+            to_members(send_piece)
         if it + 1 < ITERS:
             each_group(functools.partial(hot_of, it + 1))
         drain(near_sums.at[it], sc_recv.at[it, 0])

time: 101 us -> 103 us (1.020)
    pallas_call x1, Pallas kernels: 99.1 us -> 100 us  [local(): pl.pallas_call(functools.partial(kernel, n_band, n_member, members_here,...]
where the time goes in v6:
time: 103 us; the launch traced here: 102 us
  Pallas kernels  100 us (97%)
  local copies, waits for them, and re-layouts  1.89 us (2%)
    pallas_call x1, Pallas kernels, local(): pl.pallas_call(functools.partial(kernel, n_band, n_member, members_here,...  100 us

profile of v6, /device:TPU:1, one launch (start us, length us, event | category | flops | bytes accessed | tf_op | source)
XLA Modules:
  0.0 102.4 jit_solution(16800825269193115038)
XLA Ops:
  0.0 100.5 %shard_map.64 = f32[4,32,1024]{2,1,0:T(8,128)} custom-call(s32[2]{0:T(128)} %root_hbm.1, bf16[8,4,32,1024]{3,2,1,0:T(8,128)(2,1)} %ens_ref.1, f32[4,32,1024]{2,1,0:T(8,128)} %var_ref.1, s32[1,4096]{1,0:T(1,128)} %idx_hbm.1, f32[1,4096]{1,0:T(1,128)} %val_hbm.1, f32[1,4096]{1,0:T(1,128)} %err_hbm.1), custom_call_target="tpu_custom_call" | custom-call | tf_op jit(solution)/shard_map/pallas_call | solution.py:490
  100.5 1.9 %copy.8 = f32[4,32,1024]{2,1,0:T(8,128)} copy(f32[4,32,1024]{2,1,0:T(8,128)} %shard_map.64) | data formatting | bytes 1048576
